TPU v7x, 32 devices: a whole 2x2x4 slice. The times are simulated.
32 devices in a mesh: batch: 8 (over z, core), seq: 4 (over y, x).
Axes of the slice: x: 2, y: 2, z: 4, core: 2. Of those that a mesh axis runs over, the one named last changes fastest.
Arguments:
- frames_in: bfloat16 [8, 1024, 1024], P('batch', 'seq'), may hold values from -6 to 6
- cotangent: bfloat16 [8, 1024, 1024], P('batch', 'seq'), may hold values from -6 to 6
- levels: int32 [8], P('batch'), may hold values from 1 to 12
- lengths: int32 [8], replicated, may hold values from 256 to 1024, as said below
- token_mask: int32 [8, 1024], P('batch', 'seq'), may hold values 0 or 1
- cond_table: bfloat16 [13, 1024], replicated, may hold values from -3 to 3
- norm_gains: bfloat16 [5, 1024], replicated, may hold values from 0.25 to 1.75
- w_ffn1_up: bfloat16 [1024, 4096], replicated, may hold values from -0.1875 to 0.1875
- w_ffn1_down: bfloat16 [4096, 1024], replicated, may hold values from -0.1875 to 0.1875
- w_qkv: bfloat16 [1024, 3072], replicated, may hold values from -0.25 to 0.25
- w_out: bfloat16 [1024, 1024], replicated, may hold values from -1.5 to 1.5
- w_glu: bfloat16 [1024, 2048], replicated, may hold values from -0.1875 to 0.1875
- conv_kernel: bfloat16 [5, 1024], replicated, may hold values from -2.5 to 2.5
- bn_gain: bfloat16 [1024], replicated, may hold values from 0.25 to 1.75
- batchnorm_shift_bias: bfloat16 [1024], replicated, may hold values from -3 to 3
- w_conv_out: bfloat16 [1024, 1024], replicated, may hold values from -0.1875 to 0.1875
- w_ffn2_up: bfloat16 [1024, 4096], replicated, may hold values from -0.1875 to 0.1875
- w_ffn2_down: bfloat16 [4096, 1024], replicated, may hold values from -0.1875 to 0.1875
- running_mean: float32 [1024], replicated, may hold values from -0.24 to 0.24
- running_var: float32 [1024], replicated, may hold values from 0.02 to 0.1
Outputs:
- out: bfloat16 [8, 1024, 1024], P('batch', 'seq')
- input_grad: bfloat16 [8, 1024, 1024], P('batch', 'seq')
- cond_grad: float32 [13, 1024], P(None, 'seq')
- gains_grad: float32 [5, 1024], P(None, 'seq')
- w_ffn1_up_grad: float32 [1024, 4096], P('seq', 'batch')
- w_ffn1_down_grad: float32 [4096, 1024], P(('batch', 'seq'))
- w_qkv_grad: float32 [1024, 3072], P('seq', 'batch')
- w_out_grad: float32 [1024, 1024], P('seq', 'batch')
- w_glu_grad: float32 [1024, 2048], P('seq', 'batch')
- kernel_grad: float32 [5, 1024], P(None, 'seq')
- bn_gain_grad: float32 [1024], replicated
- bn_bias_grad: float32 [1024], replicated
- w_conv_out_grad: float32 [1024, 1024], P('seq', 'batch')
- w_ffn2_up_grad: float32 [1024, 4096], P('seq', 'batch')
- w_ffn2_down_grad: float32 [4096, 1024], P(('batch', 'seq'))
- new_running_mean: float32 [1024], replicated
- new_running_var: float32 [1024], replicated
Inputs may be any that keep to these rules, and one draw needn't show every extreme that they name: `lengths`: each item has between 256 and 1024 valid frames, a prefix of the item; at least one item is valid throughout.
All inputs are finite; a program needn't handle non-finite values. No bound on the sum of `token_mask` on one device may be relied on, other than what follows from the above.
Results may differ from a plain program's by a relative error of at most 0.024.
Values may be sent and summed in bfloat16 or wider, within the bound.
A program may use at most 448 MiB of HBM per device.

v0:
```python
import functools
import math

import jax
import jax.numpy as jnp
from jax import lax
from jax.experimental import pallas as pl
from jax.experimental.pallas import tpu as pltpu
from jax.sharding import PartitionSpec as P

MESH = pl.DeviceIdType.MESH

HEADS = 16
HD = 64


EPSILON = 1e-05
MASKED_SCORE = -1000000000.0

SEGMENTS = (
    (2, 3), (0, 2), (1, 3), (0, 1), (5, 2), (1, 2), (3, 2), (4, 3), (2, 2), (1, 1), (5, 1),
    (0, 0), (1, 0), (2, 1), (3, 1), (3, 0), (4, 2), (2, 0), (0, -1), (4, 1), (3, -1), (4, 0),
    (2, -1), (5, 0), (1, -1), (5, -1), (4, -1),
)
SWAPS = (2, 0, 4, 5, 1, 3)


def extended(array, sides, width):
    for axis, dim in sides:
        devices, length = (lax.axis_size(axis), array.shape[dim])
        up = [(i, (i + 1) % devices) for i in range(devices - 1)]
        down = [(j, i) for i, j in up]
        last = lax.slice_in_dim(array, length - width, length, axis=dim)
        leading = lax.slice_in_dim(array, 0, width, axis=dim)
        before = lax.ppermute(last, axis, up)
        after = lax.ppermute(leading, axis, down)
        array = jnp.concatenate([before, array, after], axis=dim)
    return array


def layer_norm(values, gain_row):
    centre = values - jnp.mean(values, axis=-1, keepdims=True)
    spread = jnp.mean(centre * centre, axis=-1, keepdims=True)
    return centre * lax.rsqrt(spread + EPSILON) * gain_row


def rope_tables(positions, head_size):
    half_size = head_size // 2
    inv_freqs = jnp.exp(
        jnp.arange(half_size).astype(jnp.float32) * (-2.0 * math.log(10000.0) / head_size)
    )
    angles = positions.astype(jnp.float32)[:, None] * inv_freqs[None, :]
    return (jnp.cos(angles), jnp.sin(angles))


def times_transposed(left_side, weight):
    return lax.dot_general(
        left_side, weight, (((1,), (1,)), ((), ())), preferred_element_type=jnp.float32
    )


def ffn_forward(values, gain_row, up_weight, down_weight):
    normed, ln_pull = jax.vjp(layer_norm, values, gain_row)
    lowered = normed.astype(jnp.bfloat16)
    hidden = jnp.dot(lowered, up_weight, preferred_element_type=jnp.float32)
    act_rows = (hidden * jax.nn.sigmoid(hidden)).astype(jnp.bfloat16)
    branch = jnp.dot(act_rows, down_weight, preferred_element_type=jnp.float32)
    return (values + 0.5 * branch, (ln_pull, lowered, hidden, act_rows))


def ffn_backward(grad_in, saved_state, up_weight, down_weight):
    ln_pull, lowered, hidden, act_rows = saved_state
    grad_branch = (0.5 * grad_in).astype(jnp.bfloat16)
    grad_act = times_transposed(grad_branch, down_weight)
    gate_sig = jax.nn.sigmoid(hidden)
    grad_hidden = (grad_act * gate_sig * (1.0 + hidden * (1.0 - gate_sig))).astype(jnp.bfloat16)
    grad_normed = times_transposed(grad_hidden, up_weight)
    grad_values, grad_gain = ln_pull(grad_normed)
    return (grad_in + grad_values, grad_gain, (lowered, grad_hidden), (act_rows, grad_branch))


def sum_peers(groups, batches, s, b):
    peers = [(b, lax.rem(s + k, groups)) for k in range(1, groups)]
    return peers + [(lax.rem(b + k, batches), s) for k in range(1, batches)]


def spread(pick, slots, mine, peers, span, sends, arrivals):
    slots[mine] = pick(mine)[...]
    copies = []
    for k in span:
        copies.append(
            pltpu.make_async_remote_copy(
                src_ref=pick(peers[k][1]),
                dst_ref=slots.at[mine],
                send_sem=sends.at[k],
                recv_sem=arrivals.at[k],
                device_id=peers[k],
                device_id_type=MESH,
            )
        )
        copies[-1].start()

    def finish():
        for copy in copies:
            copy.wait()
        total = slots[0]
        for i in range(1, len(copies) + 1):
            total = total + slots[i]
        return total

    return finish


def sum_kernel(groups, batches, rows_ref, total_ref, seq_slots, part, batch_slots, sends, arrivals):
    s, b = lax.axis_index("seq"), lax.axis_index("batch")
    peers = sum_peers(groups, batches, s, b)
    greet(peers)
    first = range(groups - 1)
    second = range(groups - 1, groups + batches - 2)
    part[...] = spread(lambda owner: rows_ref, seq_slots, s, peers, first, sends, arrivals)()
    total_ref[...] = spread(lambda owner: part, batch_slots, b, peers, second, sends, arrivals)()


def sum_scratch(height, width):
    groups, batches = lax.axis_size("seq"), lax.axis_size("batch")
    return [
        pltpu.VMEM((groups, height, width), jnp.float32),
        pltpu.VMEM((height, width), jnp.float32),
        pltpu.VMEM((batches, height, width), jnp.float32),
        pltpu.SemaphoreType.DMA((groups + batches - 2,)),
        pltpu.SemaphoreType.DMA((groups + batches - 2,)),
    ]


def sum_everywhere(rows, collective_id):
    groups, batches = lax.axis_size("seq"), lax.axis_size("batch")
    return pl.pallas_call(
        functools.partial(sum_kernel, groups, batches),
        out_shape=jax.ShapeDtypeStruct(rows.shape, jnp.float32),
        in_specs=[pl.BlockSpec(memory_space=pltpu.VMEM)],
        out_specs=pl.BlockSpec(memory_space=pltpu.VMEM),
        scratch_shapes=sum_scratch(*rows.shape),
        compiler_params=pltpu.CompilerParams(
            collective_id=collective_id, has_side_effects=True, vmem_limit_bytes=4 << 20
        ),
    )(rows)


def halving_steps(first_seq):
    seq_bits = [("seq", k) for k in range(lax.axis_size("seq").bit_length() - 1)]
    batch_bits = [("batch", k) for k in range(1, lax.axis_size("batch").bit_length() - 1)]
    if first_seq:
        seq_bits = seq_bits[::-1]
    return [("batch", 0)] + seq_bits + batch_bits


def relative_place(place, steps, axis):
    flips = 0
    for order, (name, bit) in enumerate(steps):
        if name == axis:
            flips = flips | (((place >> (len(steps) - 1 - order)) & 1) << bit)
    return flips


def product_kernel(steps, tall, rows, cols, group, where, left_ref, right_ref, out_ref):
    step = pl.program_id(0)
    for inner in range(group):
        place = step * group + inner
        b = where[0] ^ relative_place(place, steps, "batch")
        s = where[1] ^ relative_place(place, steps, "seq")
        if tall:
            left = left_ref[:, pl.ds(pl.multiple_of((b * lax.axis_size("seq") + s) * rows, rows), rows)]
            right = right_ref[...]
        else:
            left = left_ref[:, pl.ds(pl.multiple_of(s * rows, rows), rows)]
            right = right_ref[:, pl.ds(pl.multiple_of(b * cols, cols), cols)]
        out_ref[inner] = lax.dot_general(
            left, right, (((0,), (0,)), ((), ())), preferred_element_type=jnp.float32
        ).astype(jnp.bfloat16)


def block_products(left, right, tall, steps):
    batches, groups = lax.axis_size("batch"), lax.axis_size("seq")
    places = batches * groups
    if tall:
        rows, cols = left.shape[1] // places, right.shape[1]
    else:
        rows, cols = left.shape[1] // groups, right.shape[1] // batches
    me = jnp.stack([lax.axis_index("batch"), lax.axis_index("seq")]).astype(jnp.int32)
    if rows % 128 == 0 and cols % 128 == 0:
        group = 4
        return pl.pallas_call(
            functools.partial(product_kernel, steps, tall, rows, cols, group),
            out_shape=jax.ShapeDtypeStruct((places, rows, cols), jnp.bfloat16),
            grid_spec=pltpu.PrefetchScalarGridSpec(
                num_scalar_prefetch=1,
                grid=(places // group,),
                in_specs=[
                    pl.BlockSpec(left.shape, lambda i, where: (0, 0)),
                    pl.BlockSpec(right.shape, lambda i, where: (0, 0)),
                ],
                out_specs=pl.BlockSpec((group, rows, cols), lambda i, where: (i, 0, 0)),
            ),
            compiler_params=pltpu.CompilerParams(vmem_limit_bytes=40 << 20),
            cost_estimate=pl.CostEstimate(
                flops=2 * left.shape[0] * left.shape[1] * right.shape[1],
                bytes_accessed=2 * (left.size + right.size + left.shape[1] * right.shape[1]),
                transcendentals=0,
            ),
        )(me, left, right)
    whole = lax.dot_general(
        left, right, (((0,), (0,)), ((), ())), preferred_element_type=jnp.float32
    ).astype(jnp.bfloat16)
    if tall:
        blocks = whole.reshape(batches, groups, rows, cols)
    else:
        blocks = whole.reshape(groups, rows, batches, cols).transpose(2, 0, 1, 3)
    batch_bits, seq_bits = batches.bit_length() - 1, groups.bit_length() - 1
    blocks = blocks.reshape((2,) * (batch_bits + seq_bits) + (rows, cols))
    dims = []
    for name, bit in steps:
        dim = batch_bits - 1 - bit if name == "batch" else batch_bits + seq_bits - 1 - bit
        mine = (me[0] if name == "batch" else me[1]) >> bit & 1
        blocks = jnp.where(mine == 1, jnp.flip(blocks, dim), blocks)
        dims.append(dim)
    return blocks.transpose(*dims, len(dims), len(dims) + 1).reshape(places, rows, cols)


def owned_sum(left, right, tall, first_seq):
    steps = halving_steps(first_seq)
    blocks = block_products(left, right, tall, steps)
    for axis, bit in steps:
        half = blocks.shape[0] // 2
        pairs = [(i, i ^ (1 << bit)) for i in range(lax.axis_size(axis))]
        arrived = lax.ppermute(blocks[half:], axis, pairs)
        total = blocks[:half].astype(jnp.float32) + arrived.astype(jnp.float32)
        blocks = total.astype(jnp.bfloat16) if half > 1 else total
    return blocks[0]


def attend_kernel(groups, heads, side, *refs):
    refs = list(refs)

    def take(count):
        taken = refs[:count]
        del refs[:count]
        return taken

    length_ref, qkv_ref, cos_ref, sin_ref = take(4)
    side_in = take(len(side.inputs))
    whole_ref, out_ref = take(2)
    side_out = take(len(side.outs))
    stage, result, sends, arrivals, out_sends, out_arrivals, own_sem = take(7)
    s, b = lax.axis_index("seq"), lax.axis_index("batch")
    frames = qkv_ref.shape[0]
    total_frames = whole_ref.shape[0]
    block = heads * 3 * HD
    width = heads * HD
    parts = stage.shape[0]
    span, narrow = block // parts, width // parts
    greet_seq(groups, s, b, side)
    side.start(side_in, side_out, refs, s, b)

    def rows_of(place):
        return pl.ds(pl.multiple_of(place * frames, frames), frames)

    def heads_copy(target, sender, part):
        return pltpu.make_async_remote_copy(
            src_ref=stage.at[part, target],
            dst_ref=whole_ref.at[rows_of(sender), pl.ds(part * span, span)],
            send_sem=sends.at[part, target],
            recv_sem=arrivals.at[part, sender],
            device_id=(b, target),
            device_id_type=MESH,
        )

    columns = range(0, groups * block, 128)
    for column in sorted(columns, key=lambda c: (c % block // span if parts > 1 else 0, c)):
        pattern = (column // 128) % 3
        values = qkv_ref[:, column : column + 128]
        turned = (values * cos_ref[pattern] + partner_lanes(values) * sin_ref[pattern]).astype(
            jnp.bfloat16
        )
        start = column
        while start < column + 128:
            place, part = start // block, start % block // span
            first = place * block + part * span
            end = min(column + 128, first + span)
            stage[part, place, :, start - first : end - first] = turned[
                :, start - column : end - column
            ]
            if end == first + span:

                @pl.when(s != place)
                def _():
                    heads_copy(place, s, part).start()

                @pl.when(s == place)
                def _():
                    whole_ref[rows_of(s), part * span : (part + 1) * span] = stage[part, place]

            start = end

    valid = lax.broadcasted_iota(jnp.int32, (1, total_frames), 1) < length_ref[0]

    def out_place(owner, part):
        if narrow % 128 == 0:
            start = pl.multiple_of(owner * width + part * narrow, 128)
            return out_ref.at[:, pl.ds(start, narrow)]
        return out_ref.at[owner]

    def result_copy(target, sender, part):
        return pltpu.make_async_remote_copy(
            src_ref=result.at[part, target],
            dst_ref=out_place(sender, part),
            send_sem=out_sends.at[part, target],
            recv_sem=out_arrivals.at[part, sender],
            device_id=(b, target),
            device_id_type=MESH,
        )

    owns = []
    for part in range(parts):
        for k in range(1, groups):
            heads_copy(s, lax.rem(s + k, groups), part).wait_recv()

        def one_block(k, carry, part=part):
            place = lax.rem(s + k, groups)
            for h in range(heads // parts):
                base = part * span + h * 3 * HD
                query = whole_ref[rows_of(place), base : base + HD]
                key = whole_ref[:, base + HD : base + 2 * HD]
                value = whole_ref[:, base + 2 * HD : base + 3 * HD]
                scores = times_transposed(query, key)
                scores = jnp.where(valid, scores, MASKED_SCORE)
                exp_scores = jnp.exp(scores - jnp.max(scores, axis=-1, keepdims=True))
                share = 1.0 / jnp.sum(exp_scores, axis=-1, keepdims=True)
                probs = (exp_scores * share).astype(jnp.bfloat16)
                mixed = jnp.dot(probs, value, preferred_element_type=jnp.float32)
                result[part, place, :, h * HD : (h + 1) * HD] = mixed.astype(jnp.bfloat16)

            @pl.when(k < groups)
            def _():
                result_copy(place, s, part).start()

            return carry

        lax.fori_loop(1, groups + 1, one_block, 0)
        owns.append(pltpu.make_async_copy(result.at[part, s], out_place(s, part), own_sem.at[part]))
        owns[-1].start()
    for part in range(parts):
        for k in range(1, groups):
            other = lax.rem(s + k, groups)
            heads_copy(other, s, part).wait_send()
            result_copy(other, s, part).wait_send()
            result_copy(s, other, part).wait_recv()
    for own in owns:
        own.wait()
    side.wait()


def greet_seq(groups, s, b, side):
    greet([(b, lax.rem(s + k, groups)) for k in range(1, groups)] + side.peers(s, b))


def partner_lanes(values):
    lanes = lax.broadcasted_iota(jnp.int32, values.shape, 1)
    return jnp.where(
        lanes % HD < HD // 2,
        pltpu.roll(values, 128 - HD // 2, 1),
        pltpu.roll(values, HD // 2, 1),
    )


def attend(qkv_rows, length, cosine, sine, side):
    groups = lax.axis_size("seq")
    frames = qkv_rows.shape[0]
    heads = HEADS // groups
    width = heads * HD
    signs = jnp.where(jnp.arange(HD) < HD // 2, -1.0, 1.0)
    cos_head = jnp.concatenate([cosine, cosine], axis=1)
    sin_head = jnp.concatenate([sine, sine], axis=1) * signs
    ones, zeros = jnp.ones_like(cos_head), jnp.zeros_like(cos_head)
    cos_pair = jnp.concatenate([cos_head * 0.125, cos_head, ones] * 2, axis=1)
    sin_pair = jnp.concatenate([sin_head * 0.125, sin_head, zeros] * 2, axis=1)
    cos_three = jnp.stack([cos_pair[:, 128 * i : 128 * (i + 1)] for i in range(3)])
    sin_three = jnp.stack([sin_pair[:, 128 * i : 128 * (i + 1)] for i in range(3)])
    parts = heads // 2 if heads % 2 == 0 else 1
    direct = width // parts % 128 == 0
    out_shape = (frames, groups * width) if direct else (groups, frames, width)
    total = frames * groups
    vmem = pl.BlockSpec(memory_space=pltpu.VMEM)
    whole, out, *brought = pl.pallas_call(
        functools.partial(attend_kernel, groups, heads, side),
        out_shape=(
            jax.ShapeDtypeStruct((total, 3 * width), jnp.bfloat16),
            jax.ShapeDtypeStruct(out_shape, jnp.bfloat16),
            *side.outs,
        ),
        in_specs=[pl.BlockSpec(memory_space=pltpu.SMEM), vmem, vmem, vmem]
        + [pl.BlockSpec(memory_space=pl.ANY)] * len(side.inputs),
        out_specs=(vmem, *[pl.BlockSpec(memory_space=pl.ANY)] * (1 + len(side.outs))),
        scratch_shapes=[
            pltpu.VMEM((parts, groups, frames, 3 * width // parts), jnp.bfloat16),
            pltpu.VMEM((parts, groups, frames, width // parts), jnp.bfloat16),
            pltpu.SemaphoreType.DMA((parts, groups)),
            pltpu.SemaphoreType.DMA((parts, groups)),
            pltpu.SemaphoreType.DMA((parts, groups)),
            pltpu.SemaphoreType.DMA((parts, groups)),
            pltpu.SemaphoreType.DMA((parts,)),
            *side.scratch,
        ],
        compiler_params=pltpu.CompilerParams(
            collective_id=4, has_side_effects=True, vmem_limit_bytes=20 << 20
        ),
        cost_estimate=pl.CostEstimate(
            flops=4 * heads * HD * total * total,
            bytes_accessed=4 * qkv_rows.size + 2 * total * 4 * width,
            transcendentals=heads * total * total,
        ),
    )(length.reshape(1), qkv_rows, cos_three, sin_three, *side.inputs)
    if not direct:
        out = out.transpose(1, 0, 2).reshape(frames, groups * width)
    return whole, out, brought


def attend_back_kernel(groups, heads, side, *refs):
    refs = list(refs)

    def take(count):
        taken = refs[:count]
        del refs[:count]
        return taken

    length_ref, whole_ref, grad_ref, cos_ref, sin_ref = take(5)
    side_in = take(len(side.inputs))
    (out_ref,) = take(1)
    side_out = take(len(side.outs))
    stage, grads, result, query_key, value_total = take(5)
    sends, arrivals, out_sends, out_arrivals, own_sem = take(5)
    s, b = lax.axis_index("seq"), lax.axis_index("batch")
    frames = grad_ref.shape[0]
    total_frames = whole_ref.shape[0]
    block = heads * 3 * HD
    width = heads * HD
    greet_seq(groups, s, b, side)
    side.start(side_in, side_out, refs, s, b)

    def rows_of(place):
        return pl.ds(pl.multiple_of(place * frames, frames), frames)

    def grad_copy(target, sender):
        return pltpu.make_async_remote_copy(
            src_ref=stage.at[target],
            dst_ref=grads.at[rows_of(sender)],
            send_sem=sends.at[target],
            recv_sem=arrivals.at[sender],
            device_id=(b, target),
            device_id_type=MESH,
        )

    for place in range(groups):
        stage[place] = grad_ref[:, place * width : (place + 1) * width]

        @pl.when(s != place)
        def _():
            grad_copy(place, s).start()

        @pl.when(s == place)
        def _():
            grads[rows_of(s), :] = stage[place]

    part_heads = 2 if heads % 2 == 0 else heads
    parts = heads // part_heads
    span = part_heads * 3 * HD

    def out_place(owner, part):
        if block % 128 == 0:
            start = pl.multiple_of(owner * block + part * span, 128)
            return out_ref.at[:, pl.ds(start, span)]
        return out_ref.at[owner, :, pl.ds(part * span, span)]

    def result_copy(target, sender, part):
        return pltpu.make_async_remote_copy(
            src_ref=result.at[part, rows_of(target)],
            dst_ref=out_place(sender, part),
            send_sem=out_sends.at[part, target],
            recv_sem=out_arrivals.at[part, sender],
            device_id=(b, target),
            device_id_type=MESH,
        )

    valid = lax.broadcasted_iota(jnp.int32, (total_frames, 1), 0) < length_ref[0]
    for h in range(heads):
        base = h * 3 * HD
        key = whole_ref[:, base + HD : base + 2 * HD]
        key_turned = key.T
        value = whole_ref[:, base + 2 * HD : base + 3 * HD]
        query_key[...] = jnp.zeros_like(query_key)
        value_total[...] = jnp.zeros_like(value_total)

        def one_block(k, carry, h=h, base=base, key=key, key_turned=key_turned, value=value):
            place = lax.rem(s + k, groups)
            if h == 0:

                @pl.when(k > 0)
                def _():
                    grad_copy(s, place).wait_recv()

            query = whole_ref[rows_of(place), base : base + HD]
            grad = grads[rows_of(place), h * HD : (h + 1) * HD]
            scores = jnp.where(valid, times_transposed(key, query), MASKED_SCORE)
            exp_scores = jnp.exp(scores - jnp.max(scores, axis=0, keepdims=True))
            probs = exp_scores * (1.0 / jnp.sum(exp_scores, axis=0, keepdims=True))
            value_total[...] += jnp.dot(
                probs.astype(jnp.bfloat16), grad, preferred_element_type=jnp.float32
            )
            grad_probs = times_transposed(value, grad)
            mean = jnp.sum(probs * grad_probs, axis=0, keepdims=True)
            grad_scores = (probs * (grad_probs - mean)).astype(jnp.bfloat16)
            query_key[:, HD:] += jnp.dot(grad_scores, query, preferred_element_type=jnp.float32)
            query_key[rows_of(place), :HD] = jnp.dot(
                key_turned, grad_scores, preferred_element_type=jnp.float32
            ).T
            return carry

        lax.fori_loop(0, groups, one_block, 0)
        part, inside = h // part_heads, (h % part_heads) * 3 * HD
        both = query_key[...]
        turned = both * cos_ref[...] + partner_lanes(both) * sin_ref[...]
        result[part, :, inside : inside + 2 * HD] = turned.astype(jnp.bfloat16)
        result[part, :, inside + 2 * HD : inside + 3 * HD] = value_total[...].astype(jnp.bfloat16)
        if (h + 1) % part_heads == 0:
            for k in range(1, groups):
                result_copy(lax.rem(s + k, groups), s, part).start()
    owns = []
    for part in range(parts):
        owns.append(
            pltpu.make_async_copy(
                result.at[part, rows_of(s)], out_place(s, part), own_sem.at[part]
            )
        )
        owns[-1].start()
    for k in range(1, groups):
        other = lax.rem(s + k, groups)
        grad_copy(other, s).wait_send()
        for part in range(parts):
            result_copy(other, s, part).wait_send()
            result_copy(s, other, part).wait_recv()
    for own in owns:
        own.wait()
    side.wait()


def attend_back(whole, grad_attn, length, cosine, sine, side):
    groups = lax.axis_size("seq")
    frames = grad_attn.shape[0]
    heads = HEADS // groups
    width = heads * HD
    block = 3 * width
    total = frames * groups
    signs = jnp.where(jnp.arange(HD) < HD // 2, 1.0, -1.0)
    cos_head = jnp.concatenate([cosine, cosine], axis=1)
    sin_head = jnp.concatenate([sine, sine], axis=1) * signs
    cos_both = jnp.concatenate([cos_head * 0.125, cos_head], axis=1)
    sin_both = jnp.concatenate([sin_head * 0.125, sin_head], axis=1)
    part_heads = 2 if heads % 2 == 0 else heads
    parts = heads // part_heads
    direct = block % 128 == 0
    out_shape = (frames, groups * block) if direct else (groups, frames, block)
    vmem = pl.BlockSpec(memory_space=pltpu.VMEM)
    out, *brought = pl.pallas_call(
        functools.partial(attend_back_kernel, groups, heads, side),
        out_shape=[jax.ShapeDtypeStruct(out_shape, jnp.bfloat16), *side.outs],
        in_specs=[pl.BlockSpec(memory_space=pltpu.SMEM), vmem, vmem, vmem, vmem]
        + [pl.BlockSpec(memory_space=pl.ANY)] * len(side.inputs),
        out_specs=[pl.BlockSpec(memory_space=pl.ANY)] * (1 + len(side.outs)),
        scratch_shapes=[
            pltpu.VMEM((groups, frames, width), jnp.bfloat16),
            pltpu.VMEM((total, width), jnp.bfloat16),
            pltpu.VMEM((parts, total, part_heads * 3 * HD), jnp.bfloat16),
            pltpu.VMEM((total, 2 * HD), jnp.float32),
            pltpu.VMEM((total, HD), jnp.float32),
            pltpu.SemaphoreType.DMA((groups,)),
            pltpu.SemaphoreType.DMA((groups,)),
            pltpu.SemaphoreType.DMA((parts, groups)),
            pltpu.SemaphoreType.DMA((parts, groups)),
            pltpu.SemaphoreType.DMA((parts,)),
            *side.scratch,
        ],
        compiler_params=pltpu.CompilerParams(
            collective_id=5, has_side_effects=True, vmem_limit_bytes=24 << 20
        ),
        cost_estimate=pl.CostEstimate(
            flops=10 * heads * HD * total * total,
            bytes_accessed=2 * total * 8 * width,
            transcendentals=heads * total * total,
        ),
    )(length.reshape(1), whole, grad_attn, cos_both, sin_both, *side.inputs)
    if not direct:
        out = out.transpose(1, 0, 2).reshape(frames, groups * block)
    return out, brought


def flipped(index, places):
    for bit, flip in places:
        mine = lax.rem(index // (1 << bit), 2)
        index = index + flip * (1 - 2 * mine) * (1 << bit)
    return index


def place_of(place, steps, axis, index):
    flips = []
    for order, (name, bit) in enumerate(steps):
        if name == axis:
            flips.append((bit, lax.rem(place // (1 << (len(steps) - 1 - order)), 2)))
    return flipped(index, flips)


class Job:
    def __init__(self, parts, tall, order, far=None, gathered=None):
        self.parts, self.tall, self.far, self.gathered = parts, tall, far, gathered
        self.batches, self.groups = lax.axis_size("batch"), lax.axis_size("seq")
        bits = {
            "x": [("seq", 0)],
            "y": [("seq", k) for k in range(1, self.groups.bit_length() - 1)],
            "1": [("batch", 1)],
            "2": [("batch", k) for k in range(2, self.batches.bit_length() - 1)],
        }
        letters = order if far is None else order.replace("1", "")
        self.steps = [step for letter in letters for step in bits[letter]]
        self.sharing = 2 if far is None else 4
        self.spans = self.batches // self.sharing
        self.levels = len(self.steps)
        self.half = 1 << (self.levels - 1)
        if tall:
            ((small, big),) = parts
            self.rows = big.shape[1] // (self.batches * self.groups)
            self.widths = [small.shape[1]]
        else:
            self.rows = parts[0][0].shape[1] // self.groups
            self.widths = [big.shape[1] // self.batches for _, big in parts]
        self.cols = sum(self.widths)
        self.near_pieces = len(parts) * (self.sharing // 2 + self.spans)
        self.far_pieces = len(parts) * (self.sharing // 2 + (self.sharing - 1) * self.spans)
        if gathered is not None:
            self.near_pieces += 3
            self.far_pieces -= 3 * self.spans

    def fits(self):
        return self.rows % 128 == 0 and all(width % 128 == 0 for width in self.widths)

    def operands(self):
        extra = [array for array in (self.far, self.gathered) if array is not None]
        return [array for part in self.parts for array in part] + extra

    def flops(self):
        return sum(2 * small.size * big.shape[1] for small, big in self.parts)

    def operand_scratch(self):
        scratch, sharing = [], self.sharing
        for small, big in self.parts:
            frames = sharing * small.shape[0]
            scratch.append(pltpu.VMEM((frames, small.shape[1]), jnp.bfloat16))
            scratch.append(pltpu.VMEM((frames, big.shape[1] // sharing), jnp.bfloat16))
        return scratch + [
            pltpu.SemaphoreType.DMA((self.near_pieces,)),
            pltpu.SemaphoreType.DMA((self.far_pieces,)),
            pltpu.SemaphoreType.DMA((self.far_pieces,)),
        ]

    def step_of(self, level):
        return self.steps[self.levels - 1 - level]


def greet(peers):
    barrier = pltpu.get_barrier_semaphore()
    for peer in peers:
        pl.semaphore_signal(barrier, inc=1, device_id=peer, device_id_type=MESH)
    pl.semaphore_wait(barrier, len(peers))


def sibling_of(s, b):
    return (b + 1 - 2 * lax.rem(b, 2), s)


def partner_of(s, b, step):
    axis, bit = step
    if axis == "seq":
        return (b, flipped(s, [(bit, 1)]))
    return (flipped(b, [(bit, 1)]), s)


def quarters(s, b, n):
    core, z = lax.rem(b, 2), lax.rem(b // 2, 2)
    mine, other = 2 * (2 * n + z), 2 * (2 * n + 1 - z)
    return [
        (sibling_of(s, b), mine + 1 - core),
        ((flipped(b, [(1, 1)]), s), other + core),
        ((flipped(b, [(0, 1), (1, 1)]), s), other + 1 - core),
    ]


class Side:
    def __init__(self, rows, wide):
        self.rows, self.wide = rows, wide
        batches = lax.axis_size("batch")
        self.inputs = [*rows, *wide]
        self.outs = [jax.ShapeDtypeStruct(array.shape, array.dtype) for array in rows]
        self.outs += [
            jax.ShapeDtypeStruct((3, array.shape[0], array.shape[1] // 4), array.dtype)
            for array in wide
        ]
        self.count = len(rows) + len(wide) * 3 * (batches // 4)
        self.scratch = [pltpu.SemaphoreType.DMA((self.count,))] * 2 if self.count else []

    def peers(self, s, b):
        return [peer for peer, _ in quarters(s, b, 0)] if self.count else []

    def start(self, inputs, outs, sems, s, b):
        self.copies = []

        def send(source, place, peer):
            n = len(self.copies)
            self.copies.append(
                pltpu.make_async_remote_copy(
                    src_ref=source,
                    dst_ref=place,
                    send_sem=sems[0].at[n],
                    recv_sem=sems[1].at[n],
                    device_id=peer,
                    device_id_type=MESH,
                )
            )
            self.copies[-1].start()

        for i, array in enumerate(self.rows):
            send(inputs[i], outs[i], (flipped(b, [(1, 1)]), s))
        for i, array in enumerate(self.wide, len(self.rows)):
            batches = lax.axis_size("batch")
            span = array.shape[1] // batches
            for n in range(batches // 4):
                for k, (peer, owner) in enumerate(quarters(s, b, n)):
                    columns = pl.ds(pl.multiple_of(owner * span, 128), span)
                    send(inputs[i].at[:, columns], outs[i].at[k, :, pl.ds(n * span, span)], peer)

    def wait(self):
        for copy in self.copies:
            copy.wait()


def swap_operands(job, inputs, held, s, b):
    local, moves, lands = held[2 * len(job.parts) :]
    near, far = [], []

    def bring(source, place, peer=None):
        if peer is None:
            near.append(pltpu.make_async_copy(source, place, local.at[len(near)]))
            near[-1].start()
            return
        n = len(far)
        far.append(
            pltpu.make_async_remote_copy(
                src_ref=source,
                dst_ref=place,
                send_sem=moves.at[n],
                recv_sem=lands.at[n],
                device_id=peer,
                device_id_type=MESH,
            )
        )
        far[-1].start()

    core, z = lax.rem(b, 2), lax.rem(b // 2, 2)
    sibling = sibling_of(s, b)
    for i in range(len(job.parts)):
        small_in, big_in = inputs[2 * i : 2 * i + 2]
        small, big = held[2 * i : 2 * i + 2]
        frames = small_in.shape[0]
        span = big_in.shape[1] // job.batches

        def rows(k):
            return pl.ds(k * frames, frames)

        def columns(owner):
            return pl.ds(pl.multiple_of(owner * span, 128), span)

        bring(small_in, small.at[rows(1)], sibling)
        bring(small_in, small.at[rows(0)])
        if job.far is not None:
            bring(inputs[2], small.at[rows(3)], sibling)
            bring(inputs[2], small.at[rows(2)])
        if job.gathered is not None:
            for k in range(3):
                bring(inputs[3].at[k], big.at[rows(k + 1)])
        for n in range(job.spans):
            inside = pl.ds(n * span, span)
            if job.far is None:
                bring(big_in.at[:, columns(2 * n + 1 - core)], big.at[rows(1), inside], sibling)
                bring(big_in.at[:, columns(2 * n + core)], big.at[rows(0), inside])
                continue
            if job.gathered is None:
                for k, (peer, owner) in enumerate(quarters(s, b, n)):
                    bring(big_in.at[:, columns(owner)], big.at[rows(k + 1), inside], peer)
            bring(big_in.at[:, columns(2 * (2 * n + z) + core)], big.at[rows(0), inside])
    return near, far


def wait_operands(near, far):
    for copy in near:
        copy.wait()
    for copy in far:
        copy.wait_recv()


def block_product(job, held, part, place, s, b):
    small, big = held[2 * part : 2 * part + 2]
    span = big.shape[1] // job.spans
    row = place_of(place, job.steps, "seq", s)
    col = place_of(place, job.steps, "batch", b) // job.sharing
    if job.tall:
        left = big[:, pl.ds(pl.multiple_of(col * span + row * job.rows, 128), job.rows)]
        right = small[...]
    else:
        left = small[:, pl.ds(pl.multiple_of(row * job.rows, 128), job.rows)]
        right = big[:, pl.ds(pl.multiple_of(col * span, 128), span)]
    return lax.dot_general(
        left, right, (((0,), (0,)), ((), ())), preferred_element_type=jnp.float32
    )


def columns_of(job, part):
    start = sum(job.widths[:part])
    return slice(start, start + job.widths[part])


def scatter_kernel(jobs, sequence, *refs):
    refs = list(refs)

    def take(count):
        taken = refs[:count]
        del refs[:count]
        return taken

    inputs = [take(len(job.operands())) for job in jobs]
    (rows_ref,) = take(1)
    outs = [take(len(job.parts)) for job in jobs]
    (small_total,) = take(1)
    scratch = [(take(2 * len(job.parts) + 3), *take(4)) for job in jobs]
    seq_slots, part_sum, batch_slots, small_sends, small_arrivals = take(5)
    batches, groups = jobs[0].batches, jobs[0].groups
    s, b = lax.axis_index("seq"), lax.axis_index("batch")
    peers = sum_peers(groups, batches, s, b)
    greet(peers)

    def slot_of(job, place):
        return lax.rem(place, job.half)

    def copy_of(i, place, level):
        job = jobs[i]
        _, sending, arrived, sends, recvs = scratch[i]
        return pltpu.make_async_remote_copy(
            src_ref=sending.at[slot_of(job, place)],
            dst_ref=arrived.at[place - 1],
            send_sem=sends.at[slot_of(job, place)],
            recv_sem=recvs.at[place - 1],
            device_id=partner_of(s, b, job.step_of(level)),
            device_id_type=MESH,
        )

    works = {i: swap_operands(jobs[i], inputs[i], scratch[i][0], s, b) for i in SWAPS}

    def columns(owner):
        width = part_sum.shape[1]
        return rows_ref.at[:, pl.ds(pl.multiple_of(owner * width, 128), width)]

    over_seq = spread(
        columns, seq_slots, s, peers, range(groups - 1), small_sends, small_arrivals
    )

    def block_sums(i, place, level):
        job = jobs[i]
        held, _, arrived = scratch[i][:3]
        for m in range(job.levels - 1, level, -1):
            copy_of(i, (1 << m) + place, m).wait_recv()
        totals = []
        for part in range(len(job.parts)):
            total = block_product(job, held, part, place, s, b)
            for m in range(job.levels - 1, level, -1):
                came = arrived[(1 << m) + place - 1, :, columns_of(job, part)]
                total = total + came.astype(jnp.float32)
            totals.append(total)
        return totals

    def send_block(i, place, level):
        job = jobs[i]
        totals = block_sums(i, place, level)
        if level < job.levels - 1:
            copy_of(i, place + job.half, job.levels - 1).wait_send()
        for part, total in enumerate(totals):
            scratch[i][1][slot_of(job, place), :, columns_of(job, part)] = total.astype(jnp.bfloat16)
        copy_of(i, place, level).start()

    ready = set()
    over_batch = None
    for i, level in sequence:
        job = jobs[i]
        if i not in ready:
            ready.add(i)
            wait_operands(*works[i])
        if level < 0:
            for part, total in enumerate(block_sums(i, 0, -1)):
                outs[i][part][...] = total
            continue

        def one_place(j, carry, level=level, i=i):
            send_block(i, (2 << level) - 1 - j, level)
            return carry

        lax.fori_loop(0, 1 << level, one_place, 0)
        if over_batch is None:
            part_sum[...] = over_seq()
            over_batch = spread(
                lambda owner: part_sum,
                batch_slots,
                b,
                peers,
                range(groups - 1, groups + batches - 2),
                small_sends,
                small_arrivals,
            )
    small_total[...] = over_batch()
    for i, job in enumerate(jobs):
        for copy in works[i][1]:
            copy.wait_send()
        copy_of(i, job.half, job.levels - 1).wait_send()
        for level in range(job.levels - 1):

            def one_wait(j, carry, level=level, i=i):
                copy_of(i, (1 << level) + j, level).wait_send()
                return carry

            lax.fori_loop(0, 1 << level, one_wait, 0)


def pass_kernel(count, *refs):
    for source, target in zip(refs[:count], refs[count:]):
        target[...] = source[...]


def scatter_sums(jobs, sequence, rows, collective_id):
    height, width = rows.shape
    width = width // jobs[0].groups
    if width % 128 or not all(job.fits() for job in jobs):
        total = sum_everywhere(rows, collective_id)
        share = lax.dynamic_slice_in_dim(total, lax.axis_index("seq") * width, width, axis=1)
        sums = [
            [
                owned_sum(*((big, small) if job.tall else (small, big)), job.tall, job.tall)
                for small, big in job.parts
            ]
            for job in jobs
        ]
        return sums, share
    scratch, operands, outs = [], [], []
    for job in jobs:
        block = (job.rows, job.cols)
        scratch += job.operand_scratch()
        scratch += [
            pltpu.VMEM((job.half, *block), jnp.bfloat16),
            pltpu.VMEM((2 * job.half - 1, *block), jnp.bfloat16),
            pltpu.SemaphoreType.DMA((job.half,)),
            pltpu.SemaphoreType.DMA((2 * job.half - 1,)),
        ]
        operands += job.operands()
        outs += [jax.ShapeDtypeStruct((job.rows, width), jnp.float32) for width in job.widths]
    vmem = pl.BlockSpec(memory_space=pltpu.VMEM)
    *results, share = pl.pallas_call(
        functools.partial(scatter_kernel, jobs, sequence),
        out_shape=[*outs, jax.ShapeDtypeStruct((height, width), jnp.float32)],
        in_specs=[pl.BlockSpec(memory_space=pl.ANY)] * len(operands) + [vmem],
        out_specs=[vmem] * (len(outs) + 1),
        scratch_shapes=scratch + sum_scratch(height, width),
        compiler_params=pltpu.CompilerParams(
            collective_id=collective_id, has_side_effects=True, vmem_limit_bytes=60 << 20
        ),
        cost_estimate=pl.CostEstimate(
            flops=sum(job.flops() for job in jobs), bytes_accessed=400 << 20, transcendentals=0
        ),
    )(*operands, rows)
    passes = 4
    specs = [pl.BlockSpec((out.shape[0] // passes, out.shape[1]), lambda i: (i, 0)) for out in outs]
    results = list(
        pl.pallas_call(
            functools.partial(pass_kernel, len(outs)),
            out_shape=outs,
            grid=(passes,),
            in_specs=specs,
            out_specs=specs,
            compiler_params=pltpu.CompilerParams(vmem_limit_bytes=60 << 20),
        )(*results)
    )
    return [[results.pop(0) for _ in job.parts] for job in jobs], share


def shards(
    frames_in,
    cotangent,
    levels,
    lengths,
    token_mask,
    cond_table,
    norm_gains,
    w_ffn1_up,
    w_ffn1_down,
    w_qkv,
    w_out,
    w_glu,
    conv_kernel,
    bn_gain,
    batchnorm_shift_bias,
    w_conv_out,
    w_ffn2_up,
    w_ffn2_down,
    running_mean,
    running_var,
):
    frames = frames_in.shape[1]
    model_width = frames_in.shape[2]
    ff_width = w_ffn1_up.shape[1]
    groups = lax.axis_size("seq")
    batches = lax.axis_size("batch")
    seq_index = lax.axis_index("seq")
    item_index = lax.axis_index("batch")
    seq_length = frames * groups
    level_count = cond_table.shape[0] - 1
    cond_rows = cond_table.astype(jnp.float32)
    gain_rows = norm_gains.astype(jnp.float32)
    level_hot = (jnp.arange(level_count) == levels[0] - 1).astype(jnp.float32)
    level_vector = jnp.sum(level_hot[:, None] * cond_rows[:level_count], axis=0)
    mask_column = token_mask[0].astype(jnp.float32)[:, None]
    start_rows = (
        frames_in[0].astype(jnp.float32)
        + level_vector[None, :]
        + mask_column * cond_rows[level_count][None, :]
    )
    length = lax.dynamic_slice_in_dim(lengths, item_index, 1)[0]
    positions = seq_index * frames + jnp.arange(frames)
    unpadded_rows = (positions < length).astype(jnp.float32)[:, None]
    rows_one, ffn1_state = ffn_forward(start_rows, gain_rows[0], w_ffn1_up, w_ffn1_down)
    normed_attn, attn_pull = jax.vjp(layer_norm, rows_one, gain_rows[1])
    attn_in = normed_attn.astype(jnp.bfloat16)
    qkv_rows = jnp.dot(attn_in, w_qkv, preferred_element_type=jnp.float32)
    cosine, sine_table = rope_tables(positions, HD)
    fit = (
        model_width // groups % 128 == 0
        and model_width // batches % 128 == 0
        and ff_width // (groups * batches) % 128 == 0
    )
    side = Side([ffn1_state[1], attn_in] if fit else [], [])
    whole_heads, attn_out, brought = attend(qkv_rows, length, cosine, sine_table, side)
    far_ffn1, far_attn = brought if fit else (None, None)
    rows_two = rows_one + jnp.dot(attn_out, w_out, preferred_element_type=jnp.float32)
    normed_conv, conv_pull = jax.vjp(layer_norm, rows_two, gain_rows[2])
    conv_in = normed_conv.astype(jnp.bfloat16)
    glu_pre = jnp.dot(conv_in, w_glu, preferred_element_type=jnp.float32)
    up_half = glu_pre[:, :model_width]
    glu_sig = jax.nn.sigmoid(glu_pre[:, model_width:])
    glu_low = (up_half * glu_sig * unpadded_rows).astype(jnp.bfloat16)
    taps = conv_kernel.shape[0]
    half_size = taps // 2
    kernel_rows = conv_kernel.astype(jnp.float32)
    padded = extended(glu_low, (("seq", 0),), half_size)
    convolved_rows = jnp.zeros((frames, model_width), jnp.float32)
    for tap_index in range(taps):
        convolved_rows = (
            convolved_rows + kernel_rows[tap_index] * padded[tap_index : tap_index + frames]
        )
    sum_rows = jnp.sum(convolved_rows * unpadded_rows, axis=0)
    sum_squares = jnp.sum(convolved_rows * convolved_rows * unpadded_rows, axis=0)
    totals = sum_everywhere(jnp.stack([sum_rows, sum_squares]), 1)
    total_sum, total_squares = totals[0], totals[1]
    count_of_frames = jnp.sum(lengths).astype(jnp.float32)
    batchnorm_frame_mean = total_sum / count_of_frames
    bn_var = total_squares / count_of_frames - batchnorm_frame_mean * batchnorm_frame_mean
    batchnorm_inverse_deviation = lax.rsqrt(bn_var + EPSILON)
    batchnorm_scale_factor = bn_gain.astype(jnp.float32)
    normalized_rows = (convolved_rows - batchnorm_frame_mean) * batchnorm_inverse_deviation
    batchnorm_input_rows = normalized_rows * batchnorm_scale_factor + batchnorm_shift_bias.astype(
        jnp.float32
    )
    bn_sig = jax.nn.sigmoid(batchnorm_input_rows)
    conv_act = (batchnorm_input_rows * bn_sig).astype(jnp.bfloat16)
    rows_three = rows_two + jnp.dot(conv_act, w_conv_out, preferred_element_type=jnp.float32)
    rows_four, ffn2_state = ffn_forward(rows_three, gain_rows[3], w_ffn2_up, w_ffn2_down)
    normed_out, out_pull = jax.vjp(layer_norm, rows_four, gain_rows[4])
    out_rows = normed_out.astype(jnp.bfloat16)
    grad_four, grad_gain_four = out_pull(cotangent[0].astype(jnp.float32))
    grad_three, grad_gain_three, ffn2_up_pair, ffn2_down_pair = ffn_backward(
        grad_four, ffn2_state, w_ffn2_up, w_ffn2_down
    )
    grad_r2 = grad_three.astype(jnp.bfloat16)
    batchnorm_gradient = (
        times_transposed(grad_r2, w_conv_out)
        * bn_sig
        * (1.0 + batchnorm_input_rows * (1.0 - bn_sig))
    )
    gradient_totals = sum_everywhere(
        jnp.stack(
            [
                jnp.sum(batchnorm_gradient, axis=0),
                jnp.sum(batchnorm_gradient * normalized_rows, axis=0),
            ]
        ),
        2,
    )
    gradient_sum_total, gradient_normalized_sum = gradient_totals[0], gradient_totals[1]
    grad_conv = (
        batchnorm_scale_factor
        * batchnorm_inverse_deviation
        * (
            batchnorm_gradient
            - unpadded_rows
            * (gradient_sum_total + normalized_rows * gradient_normalized_sum)
            / count_of_frames
        )
    ).astype(jnp.bfloat16)
    grad_pad = extended(grad_conv, (("seq", 0),), half_size)
    grad_glu = jnp.zeros((frames, model_width), jnp.float32)
    kernel_terms = []
    for tap_index in range(taps):
        offset = 2 * half_size - tap_index
        grad_glu = grad_glu + kernel_rows[tap_index] * grad_pad[offset : offset + frames]
        kernel_terms.append(
            jnp.einsum(
                "fd,fd->d",
                padded[tap_index : tap_index + frames],
                grad_conv,
                preferred_element_type=jnp.float32,
            )
        )
    kernel_grads = jnp.stack(kernel_terms, axis=0)
    grad_glu = grad_glu * unpadded_rows
    grad_gl = jnp.concatenate(
        [grad_glu * glu_sig, grad_glu * up_half * glu_sig * (1.0 - glu_sig)], axis=1
    ).astype(jnp.bfloat16)
    grad_conv_in, grad_gain_two = conv_pull(times_transposed(grad_gl, w_glu))
    grad_two = grad_three + grad_conv_in
    grad_r = grad_two.astype(jnp.bfloat16)
    grad_attn_out = times_transposed(grad_r, w_out).astype(jnp.bfloat16)
    cos_all, sin_all = rope_tables(jnp.arange(seq_length), HD)
    side = Side([ffn2_up_pair[0]] if fit else [], [ffn2_up_pair[1]] if fit else [])
    grad_qkv, brought = attend_back(whole_heads, grad_attn_out, length, cos_all, sin_all, side)
    far_ffn2, gathered = brought if fit else (None, None)
    grad_attn_part, grad_gain_one = attn_pull(times_transposed(grad_qkv, w_qkv))
    grad_one = grad_two + grad_attn_part
    grad_zero, grad_gain_zero, ffn1_up_pair, ffn1_down_pair = ffn_backward(
        grad_one, ffn1_state, w_ffn1_up, w_ffn1_down
    )
    column_total = jnp.sum(grad_zero, axis=0)
    cond_grad_rows = jnp.concatenate(
        [
            level_hot[:, None] * column_total[None, :],
            jnp.sum(mask_column * grad_zero, axis=0)[None, :],
        ],
        axis=0,
    )
    gain_grads = jnp.stack(
        [grad_gain_zero, grad_gain_one, grad_gain_two, grad_gain_three, grad_gain_four], axis=0
    )
    small_rows = jnp.concatenate([gain_grads, cond_grad_rows, kernel_grads], axis=0)
    small_rows = jnp.pad(small_rows, ((0, -small_rows.shape[0] % 8), (0, 0)))
    jobs = [
        Job([ffn2_up_pair], False, "1yx2", far_ffn2, gathered),
        Job([ffn2_down_pair[::-1]], True, "y12x"),
        Job([(conv_in, grad_gl), (attn_out, grad_r), (conv_act, grad_r2)], False, "xy12"),
        Job([(attn_in, grad_qkv)], False, "1xy2", far_attn),
        Job([ffn1_down_pair[::-1]], True, "xy12"),
        Job([ffn1_up_pair], False, "12xy", far_ffn1),
    ]
    sums, small_piece = scatter_sums(jobs, SEGMENTS, small_rows, 7)
    cond_end = 5 + level_count + 1
    new_mean = 0.9 * running_mean + 0.1 * batchnorm_frame_mean
    new_var = 0.9 * running_var + 0.1 * bn_var * count_of_frames / (count_of_frames - 1.0)
    return (
        out_rows[None],
        grad_zero.astype(jnp.bfloat16)[None],
        small_piece[5:cond_end],
        small_piece[0:5],
        sums[5][0],
        sums[4][0],
        sums[3][0],
        sums[2][1],
        sums[2][0],
        small_piece[cond_end : cond_end + taps],
        gradient_normalized_sum,
        gradient_sum_total,
        sums[2][2],
        sums[0][0],
        sums[1][0],
        new_mean,
        new_var,
    )


def solution(mesh):
    in_specs = (
        P("batch", "seq", None),
        P("batch", "seq", None),
        P("batch"),
        P(),
        P("batch", "seq"),
        P(),
        P(),
        P(),
        P(),
        P(),
        P(),
        P(),
        P(),
        P(),
        P(),
        P(),
        P(),
        P(),
        P(),
        P(),
    )
    out_specs = (
        P("batch", "seq", None),
        P("batch", "seq", None),
        P(None, "seq"),
        P(None, "seq"),
        P("seq", "batch"),
        P(("batch", "seq"), None),
        P("seq", "batch"),
        P("seq", "batch"),
        P("seq", "batch"),
        P(None, "seq"),
        P(),
        P(),
        P("seq", "batch"),
        P("seq", "batch"),
        P(("batch", "seq"), None),
        P(),
        P(),
    )
    return jax.shard_map(shards, mesh=mesh, in_specs=in_specs, out_specs=out_specs, check_vma=False)
```

profile of v0, /device:TPU:0, one launch (start us, length us, event | category | flops | bytes accessed | tf_op | source)
XLA Modules:
  0.0 388.9 jit_solution(6946172040017229084)
XLA Ops:
  4.7 1.3 fusion.21
  6.0 1.4 multiply_reduce_fusion.16
  7.5 1.5 multiply_convert_fusion.13.refs_4_.refs_17_
  9.0 8.0 %multiply_convert_fusion.1 = (bf16[256,4096]{1,0:T(8,128)(2,1)S(1)}, f32[256,4096]{1,0:T(8,128)}) fusion(bf16[256,1024]{1,0:T(8,128)(2,1)S(1)} %multiply_convert_fusion.13.refs_4_.refs_17_, bf16[1024,4096]{1,0:T(8,128)(2,1)} %param.27), kind=kOutput, calls=%fused_computation.8 | convolution fusion | flops 2152726528 | bytes 15204352 | tf_op jit(solution)/shard_map/dot_general | solution.py:65
  17.0 3.3 fusion.52
  20.4 1.5 multiply_reduce_fusion.15
  23.1 1.4 multiply_convert_fusion.12.refs_5_.refs_12_
  24.6 4.8 %fusion.56.refs_1_ = f32[256,3072]{1,0:T(8,128)S(1)} fusion(bf16[256,1024]{1,0:T(8,128)(2,1)S(1)} %multiply_convert_fusion.12.refs_5_.refs_12_, bf16[1024,3072]{1,0:T(8,128)(2,1)} %param.29), kind=kOutput, calls=%fused_computation.193 | convolution fusion | flops 1610612736 | bytes 9961472 | tf_op jit(solution)/shard_map/dot_general | solution.py:1053
  30.6 32.7 %shard_map.323 = (bf16[1024,768]{1,0:T(8,128)(2,1)S(1)}, bf16[256,1024]{1,0:T(8,128)(2,1)S(1)}, bf16[256,1024]{1,0:T(8,128)(2,1)S(1)}, bf16[256,1024]{1,0:T(8,128)(2,1)S(1)}) custom-call(s32[1]{0:T(128)} %dynamic_slice.3.refs_0_, f32[256,3072]{1,0:T(8,128)S(1)} %fusion.56.refs_1_, f32[3,256,128]{2,1,0:T(8,128)S(1)} %pad_maximum_fusion.7.refs_2_, ...), custom_call_target="tpu_custom_call" | custom-call | flops 1073741824 | bytes 5242880 | tf_op jit(solution)/shard_map/pallas_call | solution.py:393
  63.3 3.0 fusion.53
  70.6 4.5 %collective-permute-start = (bf16[2,1024]{1,0:T(2,128)(2,1)S(1)}, bf16[2,1024]{1,0:T(2,128)(2,1)S(1)}, u32[]{:S(2)}, u32[]{:S(2)}) collective-permute-start(bf16[2,1024]{1,0:T(2,128)(2,1)S(1)} %get-tuple-element.117), channel_id=1, source_target_pairs={{0,1},{1,2},{2,3},{4,5},{5,6},{6,7},{8,9},{9,10},{10,11},{12,13},{... | collective-permute-start | bytes 12296 | tf_op jit(solution)/shard_map/ppermute | solution.py:35
  75.2 1.9 multiply_sine_fusion
  79.3 3.5 multiply_reduce_fusion.13
  82.8 12.7 %shard_map.324 = f32[2,1024]{1,0:T(2,128)S(1)} custom-call(f32[2,1024]{1,0:T(2,128)S(1)} %pad_maximum_fusion.9.rows_ref), custom_call_target="tpu_custom_call" | custom-call | tf_op jit(solution)/shard_map/pallas_call | solution.py:137
  95.9 2.2 fusion.54
  98.6 8.2 %multiply_convert_fusion = (bf16[256,4096]{1,0:T(8,128)(2,1)S(1)}, f32[256,4096]{1,0:T(8,128)}) fusion(bf16[256,1024]{1,0:T(8,128)(2,1)S(1)} %multiply_convert_fusion.8.refs_5_.refs_0_, bf16[1024,4096]{1,0:T(8,128)(2,1)} %param.36), kind=kOutput, calls=%fused_computation.6 | convolution fusion | flops 2152726528 | bytes 15204352 | tf_op jit(solution)/shard_map/dot_general | solution.py:65
  106.9 2.5 fusion.55
  111.5 13.7 %fusion.3.refs_6_.refs_1_ = bf16[256,4096]{1,0:T(8,128)(2,1)S(1)} fusion(bf16[256,1024]{1,0:T(8,128)(2,1)S(1)} %multiply_convert_fusion.6.refs_4_, bf16[4096,1024]{1,0:T(8,128)(2,1)S(1)} %bitcast.190, f32[256,4096]{1,0:T(8,128)} %get-tuple-element.152), kind=kOutput, calls=%fused_computation.5 | convolution fusion | flops 2156920832 | bytes 15204352 | tf_op jit(solution)/shard_map/dot_general | solution.py:57
  125.3 7.0 %multiply_reduce_fusion.1 = (f32[1024]{0:T(1024)S(1)}, f32[256]{0:T(256)S(1)}, f32[256,1024]{1,0:T(8,128)S(1)}) fusion(f32[256,1024]{1,0:T(8,128)S(1)} %get-tuple-element.150, f32[256]{0:T(256)S(1)} %fusion.36, f32[256]{0:T(256)S(1)} %broadcast_multiply_fusion.5, f32[1024]{0:T(1024)S(1)} %bitcast.154, bf16[256,4096]{1,0:T(8,128)(2,1)S(1)} %fusion.3.refs_6_.refs_1_, ...), kind=kOutput, calls=%fused_computation.48 | convolution fusion | flops 2149317376 | bytes 12594176 | tf_op jit(solution)/shard_map/dot_general | solution.py:57
  134.2 9.2 %shard_map.325 = f32[2,1024]{1,0:T(2,128)S(1)} custom-call(f32[2,1024]{1,0:T(2,128)S(1)} %pad_maximum_fusion.10.rows_ref), custom_call_target="tpu_custom_call" | custom-call | tf_op jit(solution)/shard_map/pallas_call | solution.py:137
  144.5 3.0 collective-permute-start.3
  150.0 3.0 collective-permute-done.2
  154.4 1.5 multiply_reduce_fusion.2
  158.7 46.3 %shard_map.326 = (bf16[256,3072]{1,0:T(8,128)(2,1)S(1)}, bf16[256,1024]{1,0:T(8,128)(2,1)S(1)}, bf16[3,256,1024]{2,1,0:T(8,128)(2,1)S(1)}) custom-call(s32[1]{0:T(128)} %dynamic_slice.3.refs_0_, bf16[1024,768]{1,0:T(8,128)(2,1)S(1)} %copy-done.9, bf16[256,1024]{1,0:T(8,128)(2,1)S(1)} %convolution_convert_fusion.refs_2_, ...), custom_call_target="tpu_custom_call" | custom-call | flops 2684354560 | bytes 4194304 | tf_op jit(solution)/shard_map/pallas_call | solution.py:572
  207.0 3.9 %multiply_reduce_fusion.3 = (f32[1024]{0:T(1024)S(1)}, f32[256]{0:T(256)S(1)}, f32[256,1024]{1,0:T(8,128)S(1)}) fusion(f32[256,1024]{1,0:T(8,128)} %get-tuple-element.146, f32[256]{0:T(256)S(1)} %fusion.34, f32[256]{0:T(256)S(1)} %broadcast_multiply_fusion.7, f32[1024]{0:T(1024)S(1)} %bitcast.148, bf16[256,3072]{1,0:T(8,128)(2,1)S(1)} %get-tuple-element.43.refs_13_, ...), kind=kOutput, calls=%fused_computation.50 | convolution fusion | flops 1612446464 | bytes 9972736 | tf_op jit(solution)/shard_map/dot_general | solution.py:57
  211.0 1.8 fusion.41
  213.5 3.0 fusion.2.refs_18_
  216.6 7.1 %multiply_reduce_fusion.4 = (f32[1024]{0:T(1024)S(1)}, f32[256]{0:T(256)S(1)}, f32[256,1024]{1,0:T(8,128)S(1)}) fusion(bf16[1,256,1024]{2,1,0:T(8,128)(2,1)S(1)} %copy-done.19, f32[256]{0:T(256)S(1)} %fusion.33, f32[256]{0:T(256)S(1)} %broadcast_multiply_fusion.8, f32[1024]{0:T(1024)S(1)} %bitcast.128, f32[256]{0:T(256)S(1)} %bitcast.141, ...), kind=kOutput, calls=%fused_computation.51 | convolution fusion | flops 2150365952 | bytes 12079104 | tf_op jit(solution)/shard_map/dot_general | solution.py:57
  226.3 155.4 %shard_map.327 = (f32[256,512]{1,0:T(8,128)}, f32[128,1024]{1,0:T(8,128)}, f32[256,256]{1,0:T(8,128)}, f32[256,128]{1,0:T(8,128)}, f32[256,128]{1,0:T(8,128)}, /...) custom-call(bf16[256,1024]{1,0:T(8,128)(2,1)} %copy-done.5, ...), custom_call_target="tpu_custom_call" | custom-call | flops 12348030976 | bytes 419430400 | tf_op jit(solution)/shard_map/pallas_call | solution.py:978
  381.8 1.3 slice.158
  383.1 1.3 fusion.48
  384.4 4.2 %shard_map.328 = (f32[256,512]{1,0:T(8,128)}, f32[128,1024]{1,0:T(8,128)}, f32[256,256]{1,0:T(8,128)}, f32[256,128]{1,0:T(8,128)}, f32[256,128]{1,0:T(8,128)}, /...) custom-call(f32[256,512]{1,0:T(8,128)} %get-tuple-element.49.refs_0_, ...), custom_call_target="tpu_custom_call" | custom-call | tf_op jit(solution)/shard_map/pallas_call | solution.py:994
  (201 shorter events, 29.4 us)
Async XLA Ops:
  0.7 95.2 %copy-start = (bf16[1024,1024]{1,0:T(8,128)(2,1)S(1)}, bf16[1024,1024]{1,0:T(8,128)(2,1)}, u32[]{:S(2)}) copy-start(bf16[1024,1024]{1,0:T(8,128)(2,1)} %param.35) | copy-start | bytes 6291460
  7.4 9.5 %slice-start.2 = ((s8[8388608]{0:T(1024)(128)(4,1)}), s8[4194304]{0:T(1024)(128)(4,1)S(1)}, s32[]{:S(2)}) async-start(s8[8388608]{0:T(1024)(128)(4,1)} %bitcast.191), calls=%async_computation.2 | async-start | bytes 8388608
  9.0 21.6 %copy-start.3 = (bf16[256,1024]{1,0:T(8,128)(2,1)}, bf16[256,1024]{1,0:T(8,128)(2,1)S(1)}, u32[]{:S(2)}) copy-start(bf16[256,1024]{1,0:T(8,128)(2,1)S(1)} %multiply_convert_fusion.13.refs_4_.refs_17_) | copy-start | bytes 1572868
  9.0 8.0 %copy-start.18 = (bf16[1,256,1024]{2,1,0:T(8,128)(2,1)S(1)}, bf16[1,256,1024]{2,1,0:T(8,128)(2,1)}, u32[]{:S(2)}) copy-start(bf16[1,256,1024]{2,1,0:T(8,128)(2,1)} %param.20) | copy-start | bytes 1572868
  9.0 8.0 %slice-start.3 = ((s8[8388608]{0:T(1024)(128)(4,1)}), s8[4194304]{0:T(1024)(128)(4,1)S(1)}, s32[]{:S(2)}) async-start(s8[8388608]{0:T(1024)(128)(4,1)} %bitcast.191), calls=%async_computation.3 | async-start | bytes 8388608
  30.5 32.8 %copy-start.23 = (bf16[1024,1024]{1,0:T(8,128)(2,1)S(1)}, bf16[1024,1024]{1,0:T(8,128)(2,1)}, u32[]{:S(2)}) copy-start(bf16[1024,1024]{1,0:T(8,128)(2,1)} %param.30) | copy-start | bytes 6291460
  67.6 7.6 %copy-start.31 = (bf16[5,1024]{1,0:T(8,128)(2,1)S(1)}, bf16[5,1024]{1,0:T(8,128)(2,1)}, u32[]{:S(2)}) copy-start(bf16[5,1024]{1,0:T(8,128)(2,1)} %param.32) | copy-start | bytes 30724
  68.9 8.9 %copy-start.16 = (f32[256,2048]{1,0:T(8,128)}, f32[256,2048]{1,0:T(8,128)S(1)}, u32[]{:S(2)}) copy-start(f32[256,2048]{1,0:T(8,128)S(1)} %fusion.57) | copy-start | bytes 6291460
  68.9 9.7 %copy-start.37 = (bf16[1024]{0:T(1024)(128)(2,1)S(1)}, bf16[1024]{0:T(1024)(128)(2,1)}, u32[]{:S(2)}) copy-start(bf16[1024]{0:T(1024)(128)(2,1)} %param.34) | copy-start | bytes 6148
  68.9 9.7 %copy-start.34 = (bf16[1024]{0:T(1024)(128)(2,1)S(1)}, bf16[1024]{0:T(1024)(128)(2,1)}, u32[]{:S(2)}) copy-start(bf16[1024]{0:T(1024)(128)(2,1)} %param.33) | copy-start | bytes 6148
  69.2 8.5 %copy-start.20 = (bf16[256,1024]{1,0:T(8,128)(2,1)}, bf16[256,1024]{1,0:T(8,128)(2,1)S(1)}, u32[]{:S(2)}) copy-start(bf16[256,1024]{1,0:T(8,128)(2,1)S(1)} %multiply_convert_fusion.10) | copy-start | bytes 1572868
  69.3 10.0 %collective-permute-start.1 = (bf16[2,1024]{1,0:T(2,128)(2,1)S(1)}, bf16[2,1024]{1,0:T(2,128)(2,1)S(1)}, u32[]{:S(2)}, u32[]{:S(2)}) collective-permute-start(bf16[2,1024]{1,0:T(2,128)(2,1)S(1)} %get-tuple-element.118), channel_id=1, source_target_pairs={{1,0},{2,1},{3,2},{5,4},{6,5},{7,6},{9,8},{10,9},{11,10},{13,12},{... | collective-permute-start | bytes 12296 | tf_op jit(solution)/shard_map/ppermute | solution.py:36
  70.6 8.7 %collective-permute-start = (bf16[2,1024]{1,0:T(2,128)(2,1)S(1)}, bf16[2,1024]{1,0:T(2,128)(2,1)S(1)}, u32[]{:S(2)}, u32[]{:S(2)}) collective-permute-start(bf16[2,1024]{1,0:T(2,128)(2,1)S(1)} %get-tuple-element.117), channel_id=1, source_target_pairs={{0,1},{1,2},{2,3},{4,5},{5,6},{6,7},{8,9},{9,10},{10,11},{12,13},{... | collective-permute-start | bytes 12296 | tf_op jit(solution)/shard_map/ppermute | solution.py:35
  95.9 11.0 %copy-start.22 = (bf16[256,1024]{1,0:T(8,128)(2,1)}, bf16[256,1024]{1,0:T(8,128)(2,1)S(1)}, u32[]{:S(2)}) copy-start(bf16[256,1024]{1,0:T(8,128)(2,1)S(1)} %multiply_convert_fusion.9.refs_10_) | copy-start | bytes 1572868
  98.1 8.8 %slice-start = ((s8[8388608]{0:T(1024)(128)(4,1)}), s8[4194304]{0:T(1024)(128)(4,1)S(1)}, s32[]{:S(2)}) async-start(s8[8388608]{0:T(1024)(128)(4,1)} %bitcast.189), calls=%async_computation | async-start | bytes 8388608
  98.6 60.1 %copy-start.5 = (bf16[256,1024]{1,0:T(8,128)(2,1)}, bf16[256,1024]{1,0:T(8,128)(2,1)S(1)}, u32[]{:S(2)}) copy-start(bf16[256,1024]{1,0:T(8,128)(2,1)S(1)} %multiply_convert_fusion.8.refs_5_.refs_0_) | copy-start | bytes 1572868
  98.6 8.3 %slice-start.1 = ((s8[8388608]{0:T(1024)(128)(4,1)}), s8[4194304]{0:T(1024)(128)(4,1)S(1)}, s32[]{:S(2)}) async-start(s8[8388608]{0:T(1024)(128)(4,1)} %bitcast.189), calls=%async_computation.1 | async-start | bytes 8388608
  111.5 13.7 %copy-start.30 = (bf16[256,1024]{1,0:T(8,128)(2,1)}, bf16[256,1024]{1,0:T(8,128)(2,1)S(1)}, u32[]{:S(2)}) copy-start(bf16[256,1024]{1,0:T(8,128)(2,1)S(1)} %multiply_convert_fusion.6.refs_4_) | copy-start | bytes 1572868
  125.2 33.4 %copy-start.7 = (bf16[256,4096]{1,0:T(8,128)(2,1)}, bf16[256,4096]{1,0:T(8,128)(2,1)S(1)}, u32[]{:S(2)}) copy-start(bf16[256,4096]{1,0:T(8,128)(2,1)S(1)} %fusion.3.refs_6_.refs_1_) | copy-start | bytes 6291460
  132.9 10.4 %copy-start.21 = (bf16[256,1024]{1,0:T(8,128)(2,1)S(1)}, bf16[256,1024]{1,0:T(8,128)(2,1)}, u32[]{:S(2)}) copy-start(bf16[256,1024]{1,0:T(8,128)(2,1)} %copy-done.20) | copy-start | bytes 1572868
  132.9 15.9 %copy-start.35 = (f32[1024]{0:T(1024)S(1)}, f32[1024]{0:T(1024)}, u32[]{:S(2)}) copy-start(f32[1024]{0:T(1024)} %param.38) | copy-start | bytes 12292
  133.0 16.5 %copy-start.36 = (f32[1024]{0:T(1024)S(1)}, f32[1024]{0:T(1024)}, u32[]{:S(2)}) copy-start(f32[1024]{0:T(1024)} %param.39) | copy-start | bytes 12292
  133.0 20.1 %copy-start.17 = (f32[256,2048]{1,0:T(8,128)S(1)}, f32[256,2048]{1,0:T(8,128)}, u32[]{:S(2)}) copy-start(f32[256,2048]{1,0:T(8,128)} %copy-done.16) | copy-start | bytes 6291460
  143.3 11.0 %copy-start.32 = (f32[1,1024]{1,0:T(1,128)}, f32[1,1024]{1,0:T(1,128)S(1)}, u32[]{:S(2)}) copy-start(f32[1,1024]{1,0:T(1,128)S(1)} %get-tuple-element.137) | copy-start | bytes 12292
  143.4 11.0 %copy-start.33 = (f32[1,1024]{1,0:T(1,128)}, f32[1,1024]{1,0:T(1,128)S(1)}, u32[]{:S(2)}) copy-start(f32[1,1024]{1,0:T(1,128)S(1)} %get-tuple-element.138) | copy-start | bytes 12292
  144.5 9.9 %copy-start.15 = (f32[256,1024]{1,0:T(8,128)S(1)}, f32[256,1024]{1,0:T(8,128)}, u32[]{:S(2)}) copy-start(f32[256,1024]{1,0:T(8,128)} %copy-done.14) | copy-start | bytes 3145732
  144.5 9.9 %copy-start.39 = (bf16[1024,2048]{1,0:T(8,128)(2,1)S(1)}, bf16[1024,2048]{1,0:T(8,128)(2,1)}, u32[]{:S(2)}) copy-start(bf16[1024,2048]{1,0:T(8,128)(2,1)} %param.31) | copy-start | bytes 12582916
  144.5 5.5 %collective-permute-start.3 = (bf16[2,1024]{1,0:T(2,128)(2,1)S(1)}, bf16[2,1024]{1,0:T(2,128)(2,1)S(1)}, u32[]{:S(2)}, u32[]{:S(2)}) collective-permute-start(bf16[2,1024]{1,0:T(2,128)(2,1)S(1)} %get-tuple-element.116), channel_id=1, source_target_pairs={{0,1},{1,2},{2,3},{4,5},{5,6},{6,7},{8,9},{9,10},{10,11},{12,13},{... | collective-permute-start | bytes 12296 | tf_op jit(solution)/shard_map/ppermute | solution.py:35
  147.5 5.5 %collective-permute-start.2 = (bf16[2,1024]{1,0:T(2,128)(2,1)S(1)}, bf16[2,1024]{1,0:T(2,128)(2,1)S(1)}, u32[]{:S(2)}, u32[]{:S(2)}) collective-permute-start(bf16[2,1024]{1,0:T(2,128)(2,1)S(1)} %get-tuple-element.115), channel_id=1, source_target_pairs={{1,0},{2,1},{3,2},{5,4},{6,5},{7,6},{9,8},{10,9},{11,10},{13,12},{... | collective-permute-start | bytes 12296 | tf_op jit(solution)/shard_map/ppermute | solution.py:36
  157.9 49.1 %slice-start.6 = ((s8[6291456]{0:T(1024)(128)(4,1)}), s8[4194304]{0:T(1024)(128)(4,1)S(1)}, s32[]{:S(2)}) async-start(s8[6291456]{0:T(1024)(128)(4,1)} %bitcast.195), calls=%async_computation.6 | async-start | bytes 8388608
  158.7 48.3 %slice-start.7 = ((s8[6291456]{0:T(1024)(128)(4,1)}), s8[2097152]{0:T(1024)(128)(4,1)S(1)}, s32[]{:S(2)}) async-start(s8[6291456]{0:T(1024)(128)(4,1)} %bitcast.195), calls=%async_computation.7 | async-start | bytes 4194304
  226.3 162.3 %copy-start.1 = (bf16[1024,1024]{1,0:T(8,128)(2,1)S(1)}, bf16[1024,1024]{1,0:T(8,128)(2,1)}, u32[]{:S(2)}) copy-start(bf16[1024,1024]{1,0:T(8,128)(2,1)} %param.35) | copy-start | bytes 6291460
  (25 other events, 88.6 us)
where the time goes:
time: 393 us; the launch traced here: 389 us
  Pallas kernels  260 us (66%)
  matrix products  71.4 us (18%)
  other arithmetic  30.7 us (8%)
  starting transfers between devices  10.1 us (3%)
  local copies, waits for them, and re-layouts  9.83 us (3%)
    pallas_call x1, Pallas kernels, scatter_sums(): pl.pallas_call(functools.partial(scatter_kernel, jobs, sequence), out_sha...  155 us
    pallas_call x1, Pallas kernels, attend_back(): pl.pallas_call(functools.partial(attend_back_kernel, groups, heads, side)...  46.3 us
    dot_general x8, matrix products, times_transposed(): lax.dot_general(left_side, weight, (((1,), (1,)), ((), ())), preferred_el...  38.1 us
    pallas_call x1, Pallas kernels, attend(): pl.pallas_call(functools.partial(attend_kernel, groups, heads, side), out...  32.7 us
    pallas_call x2, Pallas kernels, sum_everywhere(): pl.pallas_call(functools.partial(sum_kernel, groups, batches), out_shape=...  21.8 us
    dot_general x2, matrix products, ffn_forward(): hidden = jnp.dot(lowered, up_weight, preferred_element_type=jnp.float32)  16.2 us
  transfers between devices with their start and end apart: 4, of which 1 were waited for; matrix products, arithmetic and copies ran while one was open for 1% of the time, Pallas kernels for 0%

commit v1 on v0

--- a/solution.py
+++ b/solution.py
@@ -23,19 +23,6 @@
     (2, -1), (5, 0), (1, -1), (5, -1), (4, -1),
 )
 SWAPS = (2, 0, 4, 5, 1, 3)
-
-
-def extended(array, sides, width):
-    for axis, dim in sides:
-        devices, length = (lax.axis_size(axis), array.shape[dim])
-        up = [(i, (i + 1) % devices) for i in range(devices - 1)]
-        down = [(j, i) for i, j in up]
-        last = lax.slice_in_dim(array, length - width, length, axis=dim)
-        leading = lax.slice_in_dim(array, 0, width, axis=dim)
-        before = lax.ppermute(last, axis, up)
-        after = lax.ppermute(leading, axis, down)
-        array = jnp.concatenate([before, array, after], axis=dim)
-    return array
 
 
 def layer_norm(values, gain_row):
@@ -144,6 +131,242 @@
             collective_id=collective_id, has_side_effects=True, vmem_limit_bytes=4 << 20
         ),
     )(rows)
+
+
+def edge_copies(groups, s, b, rows_ref, before, after, tile, sends, arrivals, first):
+    up = pltpu.make_async_remote_copy(
+        src_ref=rows_ref.at[pl.ds(rows_ref.shape[0] - tile, tile)],
+        dst_ref=before,
+        send_sem=sends.at[first],
+        recv_sem=arrivals.at[first],
+        device_id=(b, lax.rem(s + 1, groups)),
+        device_id_type=MESH,
+    )
+    down = pltpu.make_async_remote_copy(
+        src_ref=rows_ref.at[pl.ds(0, tile)],
+        dst_ref=after,
+        send_sem=sends.at[first + 1],
+        recv_sem=arrivals.at[first + 1],
+        device_id=(b, lax.rem(s + groups - 1, groups)),
+        device_id_type=MESH,
+    )
+    return up, down
+
+
+def start_edges(groups, s, copies):
+    @pl.when(s < groups - 1)
+    def _():
+        for up, _ in copies:
+            up.start()
+
+    @pl.when(s > 0)
+    def _():
+        for _, down in copies:
+            down.start()
+
+
+def wait_edges_sent(groups, s, copies):
+    @pl.when(s < groups - 1)
+    def _():
+        for up, _ in copies:
+            up.wait_send()
+
+    @pl.when(s > 0)
+    def _():
+        for _, down in copies:
+            down.wait_send()
+
+
+def valid_rows(first, count, length):
+    positions = first + lax.broadcasted_iota(jnp.int32, (count, 1), 0)
+    return (positions < length).astype(jnp.float32)
+
+
+def convolve_kernel(
+    groups, batches, taps, length_ref, glu_ref, kernel_ref, out_ref, padded_ref, total_ref,
+    before, after, local, edge_sends, edge_arrivals, seq_slots, part, batch_slots, sends, arrivals,
+):
+    s, b = lax.axis_index("seq"), lax.axis_index("batch")
+    peers = sum_peers(groups, batches, s, b)
+    signal(peers)
+    frames, width = glu_ref.shape
+    padded_ref[8 : 8 + frames, :] = glu_ref[...].astype(jnp.float32)
+    wait_signals(peers)
+    edges = [edge_copies(groups, s, b, glu_ref, before, after, 16, edge_sends, edge_arrivals, 0)]
+    start_edges(groups, s, edges)
+
+    @pl.when(s > 0)
+    def _():
+        edges[0][0].wait_recv()
+        padded_ref[0:8, :] = before[8:16, :].astype(jnp.float32)
+
+    @pl.when(s == 0)
+    def _():
+        padded_ref[0:8, :] = jnp.zeros((8, width), jnp.float32)
+
+    @pl.when(s < groups - 1)
+    def _():
+        edges[0][1].wait_recv()
+        padded_ref[8 + frames :, :] = after[0:8, :].astype(jnp.float32)
+
+    @pl.when(s == groups - 1)
+    def _():
+        padded_ref[8 + frames :, :] = jnp.zeros((8, width), jnp.float32)
+
+    valid = valid_rows(s * frames, frames, length_ref[0])
+    for column in range(0, width, 128):
+        lanes = slice(column, column + 128)
+        total = jnp.zeros((frames, 128), jnp.float32)
+        for k in range(taps):
+            start = 8 - taps // 2 + k
+            total = total + kernel_ref[k : k + 1, lanes] * padded_ref[start : start + frames, lanes]
+        out_ref[:, lanes] = total
+        kept = total * valid
+        local[0:1, lanes] = jnp.sum(kept, axis=0, keepdims=True)
+        local[1:2, lanes] = jnp.sum(kept * total, axis=0, keepdims=True)
+    first, second = range(groups - 1), range(groups - 1, groups + batches - 2)
+    part[...] = spread(lambda owner: local, seq_slots, s, peers, first, sends, arrivals)()
+    total_ref[...] = spread(lambda owner: part, batch_slots, b, peers, second, sends, arrivals)()
+    wait_edges_sent(groups, s, edges)
+
+
+def convolve(glu_low, kernel_rows, length):
+    groups, batches = lax.axis_size("seq"), lax.axis_size("batch")
+    frames, width = glu_low.shape
+    taps = kernel_rows.shape[0]
+    vmem = pl.BlockSpec(memory_space=pltpu.VMEM)
+    return pl.pallas_call(
+        functools.partial(convolve_kernel, groups, batches, taps),
+        out_shape=[
+            jax.ShapeDtypeStruct((frames, width), jnp.float32),
+            jax.ShapeDtypeStruct((frames + 16, width), jnp.float32),
+            jax.ShapeDtypeStruct((2, width), jnp.float32),
+        ],
+        in_specs=[pl.BlockSpec(memory_space=pltpu.SMEM), vmem, vmem],
+        out_specs=[vmem] * 3,
+        scratch_shapes=[
+            pltpu.VMEM((16, width), jnp.bfloat16),
+            pltpu.VMEM((16, width), jnp.bfloat16),
+            pltpu.VMEM((2, width), jnp.float32),
+            pltpu.SemaphoreType.DMA((2,)),
+            pltpu.SemaphoreType.DMA((2,)),
+            *sum_scratch(2, width),
+        ],
+        compiler_params=pltpu.CompilerParams(
+            collective_id=1, has_side_effects=True, vmem_limit_bytes=8 << 20
+        ),
+    )(length.reshape(1), glu_low, kernel_rows)
+
+
+def convolve_back_kernel(
+    groups, batches, taps, length_ref, count_ref, grad_ref, conv_ref, padded_ref, kernel_ref, norm_ref,
+    out_ref, taps_ref, total_ref, edge_rows, spread_rows, local, edge_sends, edge_arrivals,
+    seq_slots, part, batch_slots, sends, arrivals,
+):
+    s, b = lax.axis_index("seq"), lax.axis_index("batch")
+    peers = sum_peers(groups, batches, s, b)
+    signal(peers)
+    frames, width = grad_ref.shape
+
+    def normalized(values, lanes):
+        return (values - norm_ref[0:1, lanes]) * norm_ref[1:2, lanes]
+
+    for column in range(0, width, 128):
+        lanes = slice(column, column + 128)
+        grads = grad_ref[:, lanes]
+        local[0:1, lanes] = jnp.sum(grads, axis=0, keepdims=True)
+        local[1:2, lanes] = jnp.sum(
+            grads * normalized(conv_ref[:, lanes], lanes), axis=0, keepdims=True
+        )
+    wait_signals(peers)
+    edges = [
+        edge_copies(
+            groups, s, b, ref, edge_rows.at[2 * i], edge_rows.at[2 * i + 1], 8,
+            edge_sends, edge_arrivals, 2 * i,
+        )
+        for i, ref in enumerate((grad_ref, conv_ref))
+    ]
+    start_edges(groups, s, edges)
+    first, second = range(groups - 1), range(groups - 1, groups + batches - 2)
+    part[...] = spread(lambda owner: local, seq_slots, s, peers, first, sends, arrivals)()
+    total_ref[...] = spread(lambda owner: part, batch_slots, b, peers, second, sends, arrivals)()
+
+    length = length_ref[0]
+    share = 1.0 / count_ref[0]
+
+    def conv_grad(grads, values, valid, lanes):
+        sums = total_ref[0:1, lanes] + normalized(values, lanes) * total_ref[1:2, lanes]
+        rows = norm_ref[2:3, lanes] * norm_ref[1:2, lanes] * (grads - valid * sums * share)
+        return rows.astype(jnp.bfloat16).astype(jnp.float32)
+
+    @pl.when(s > 0)
+    def _():
+        for up, _ in edges:
+            up.wait_recv()
+        spread_rows[0:8, :] = conv_grad(
+            edge_rows[0], edge_rows[2], valid_rows(s * frames - 8, 8, length), slice(None)
+        )
+
+    @pl.when(s == 0)
+    def _():
+        spread_rows[0:8, :] = jnp.zeros((8, width), jnp.float32)
+
+    @pl.when(s < groups - 1)
+    def _():
+        for _, down in edges:
+            down.wait_recv()
+        spread_rows[8 + frames :, :] = conv_grad(
+            edge_rows[1], edge_rows[3], valid_rows((s + 1) * frames, 8, length), slice(None)
+        )
+
+    @pl.when(s == groups - 1)
+    def _():
+        spread_rows[8 + frames :, :] = jnp.zeros((8, width), jnp.float32)
+
+    valid = valid_rows(s * frames, frames, length)
+    taps_ref[...] = jnp.zeros_like(taps_ref)
+    for column in range(0, width, 128):
+        lanes = slice(column, column + 128)
+        own = conv_grad(grad_ref[:, lanes], conv_ref[:, lanes], valid, lanes)
+        spread_rows[8 : 8 + frames, lanes] = own
+        total = jnp.zeros((frames, 128), jnp.float32)
+        for k in range(taps):
+            start = 8 + taps // 2 - k
+            total = total + kernel_ref[k : k + 1, lanes] * spread_rows[start : start + frames, lanes]
+            start = 8 - taps // 2 + k
+            taps_ref[k : k + 1, lanes] = jnp.sum(
+                padded_ref[start : start + frames, lanes] * own, axis=0, keepdims=True
+            )
+        out_ref[:, lanes] = total * valid
+    wait_edges_sent(groups, s, edges)
+
+
+def convolve_back(grads, convolved, padded, kernel_rows, norm_rows, length, count):
+    groups, batches = lax.axis_size("seq"), lax.axis_size("batch")
+    frames, width = grads.shape
+    taps = kernel_rows.shape[0]
+    vmem, smem = pl.BlockSpec(memory_space=pltpu.VMEM), pl.BlockSpec(memory_space=pltpu.SMEM)
+    return pl.pallas_call(
+        functools.partial(convolve_back_kernel, groups, batches, taps),
+        out_shape=[
+            jax.ShapeDtypeStruct((frames, width), jnp.float32),
+            jax.ShapeDtypeStruct((8, width), jnp.float32),
+            jax.ShapeDtypeStruct((2, width), jnp.float32),
+        ],
+        in_specs=[smem, smem, vmem, vmem, vmem, vmem, vmem],
+        out_specs=[vmem] * 3,
+        scratch_shapes=[
+            pltpu.VMEM((4, 8, width), jnp.float32),
+            pltpu.VMEM((frames + 16, width), jnp.float32),
+            pltpu.VMEM((2, width), jnp.float32),
+            pltpu.SemaphoreType.DMA((4,)),
+            pltpu.SemaphoreType.DMA((4,)),
+            *sum_scratch(2, width),
+        ],
+        compiler_params=pltpu.CompilerParams(
+            collective_id=2, has_side_effects=True, vmem_limit_bytes=12 << 20
+        ),
+    )(length.reshape(1), count.reshape(1), grads, convolved, padded, kernel_rows, norm_rows)
 
 
 def halving_steps(first_seq):
@@ -673,11 +896,19 @@
         return self.steps[self.levels - 1 - level]
 
 
-def greet(peers):
+def signal(peers):
     barrier = pltpu.get_barrier_semaphore()
     for peer in peers:
         pl.semaphore_signal(barrier, inc=1, device_id=peer, device_id_type=MESH)
-    pl.semaphore_wait(barrier, len(peers))
+
+
+def wait_signals(peers):
+    pl.semaphore_wait(pltpu.get_barrier_semaphore(), len(peers))
+
+
+def greet(peers):
+    signal(peers)
+    wait_signals(peers)
 
 
 def sibling_of(s, b):
@@ -1068,17 +1299,8 @@
     glu_sig = jax.nn.sigmoid(glu_pre[:, model_width:])
     glu_low = (up_half * glu_sig * unpadded_rows).astype(jnp.bfloat16)
     taps = conv_kernel.shape[0]
-    half_size = taps // 2
     kernel_rows = conv_kernel.astype(jnp.float32)
-    padded = extended(glu_low, (("seq", 0),), half_size)
-    convolved_rows = jnp.zeros((frames, model_width), jnp.float32)
-    for tap_index in range(taps):
-        convolved_rows = (
-            convolved_rows + kernel_rows[tap_index] * padded[tap_index : tap_index + frames]
-        )
-    sum_rows = jnp.sum(convolved_rows * unpadded_rows, axis=0)
-    sum_squares = jnp.sum(convolved_rows * convolved_rows * unpadded_rows, axis=0)
-    totals = sum_everywhere(jnp.stack([sum_rows, sum_squares]), 1)
+    convolved_rows, padded, totals = convolve(glu_low, kernel_rows, length)
     total_sum, total_squares = totals[0], totals[1]
     count_of_frames = jnp.sum(lengths).astype(jnp.float32)
     batchnorm_frame_mean = total_sum / count_of_frames
@@ -1105,42 +1327,14 @@
         * bn_sig
         * (1.0 + batchnorm_input_rows * (1.0 - bn_sig))
     )
-    gradient_totals = sum_everywhere(
-        jnp.stack(
-            [
-                jnp.sum(batchnorm_gradient, axis=0),
-                jnp.sum(batchnorm_gradient * normalized_rows, axis=0),
-            ]
-        ),
-        2,
-    )
+    norm_rows = jnp.stack(
+        [batchnorm_frame_mean, batchnorm_inverse_deviation, batchnorm_scale_factor], axis=0
+    )
+    grad_glu, kernel_grads, gradient_totals = convolve_back(
+        batchnorm_gradient, convolved_rows, padded, kernel_rows, norm_rows, length, count_of_frames
+    )
+    kernel_grads = kernel_grads[:taps]
     gradient_sum_total, gradient_normalized_sum = gradient_totals[0], gradient_totals[1]
-    grad_conv = (
-        batchnorm_scale_factor
-        * batchnorm_inverse_deviation
-        * (
-            batchnorm_gradient
-            - unpadded_rows
-            * (gradient_sum_total + normalized_rows * gradient_normalized_sum)
-            / count_of_frames
-        )
-    ).astype(jnp.bfloat16)
-    grad_pad = extended(grad_conv, (("seq", 0),), half_size)
-    grad_glu = jnp.zeros((frames, model_width), jnp.float32)
-    kernel_terms = []
-    for tap_index in range(taps):
-        offset = 2 * half_size - tap_index
-        grad_glu = grad_glu + kernel_rows[tap_index] * grad_pad[offset : offset + frames]
-        kernel_terms.append(
-            jnp.einsum(
-                "fd,fd->d",
-                padded[tap_index : tap_index + frames],
-                grad_conv,
-                preferred_element_type=jnp.float32,
-            )
-        )
-    kernel_grads = jnp.stack(kernel_terms, axis=0)
-    grad_glu = grad_glu * unpadded_rows
     grad_gl = jnp.concatenate(
         [grad_glu * glu_sig, grad_glu * up_half * glu_sig * (1.0 - glu_sig)], axis=1
     ).astype(jnp.bfloat16)

time: 393 us -> 388 us (0.987)
  Pallas kernels: 260 us -> 271 us
  starting transfers between devices: 10.1 us -> 0 us
  local copies, waits for them, and re-layouts: 9.83 us -> 16.6 us
  other arithmetic: 30.7 us -> 24 us
    pallas_call x2, Pallas kernels: 21.8 us -> 32.1 us  [the longest x1 17.3 us: convolve(): pl.pallas_call(functools.partial(convolve_kernel, groups, batches, taps),...]
    ppermute x4 -> x0, starting transfers between devices: 10.1 us -> none  [the longest x2 7.56 us: extended(): before = lax.ppermute(last, axis, up)]
    unnamed x106 -> x108, local copies, waits for them, and re-layouts: 3.75 us -> 10.1 us
  transfers between devices with their start and end apart: 4 -> 0, of which waited for: 1 -> 0; matrix products, arithmetic and copies ran while one was open for 1% -> 0% of each run, Pallas kernels for 0% -> 0%
where the time goes in v1:
time: 388 us; the launch traced here: 384 us
  Pallas kernels  271 us (70%)
  matrix products  69.1 us (18%)
  other arithmetic  24 us (6%)
  local copies, waits for them, and re-layouts  16.6 us (4%)
    pallas_call x1, Pallas kernels, scatter_sums(): pl.pallas_call(functools.partial(scatter_kernel, jobs, sequence), out_sha...  154 us
    pallas_call x1, Pallas kernels, attend_back(): pl.pallas_call(functools.partial(attend_back_kernel, groups, heads, side)...  47.4 us
    dot_general x8, matrix products, times_transposed(): lax.dot_general(left_side, weight, (((1,), (1,)), ((), ())), preferred_el...  36.5 us
    pallas_call x1, Pallas kernels, attend(): pl.pallas_call(functools.partial(attend_kernel, groups, heads, side), out...  32.6 us
    pallas_call x1, Pallas kernels, convolve(): pl.pallas_call(functools.partial(convolve_kernel, groups, batches, taps),...  17.3 us
    dot_general x2, matrix products, ffn_forward(): hidden = jnp.dot(lowered, up_weight, preferred_element_type=jnp.float32)  16.1 us
    pallas_call x1, Pallas kernels, convolve_back(): pl.pallas_call(functools.partial(convolve_back_kernel, groups, batches, t...  14.8 us
    unnamed x108, local copies, waits for them, and re-layouts  10.1 us

profile of v1, /device:TPU:0, one launch (start us, length us, event | category | flops | bytes accessed | tf_op | source)
XLA Modules:
  0.0 383.7 jit_solution(12379099162223698964)
XLA Ops:
  4.5 1.3 fusion.16
  5.9 1.4 multiply_reduce_fusion.13
  7.3 1.5 multiply_convert_fusion.12.refs_4_.refs_17_
  8.9 8.0 %multiply_convert_fusion.1 = (bf16[256,4096]{1,0:T(8,128)(2,1)S(1)}, f32[256,4096]{1,0:T(8,128)}) fusion(bf16[256,1024]{1,0:T(8,128)(2,1)S(1)} %multiply_convert_fusion.12.refs_4_.refs_17_, bf16[1024,4096]{1,0:T(8,128)(2,1)} %param.27), kind=kOutput, calls=%fused_computation.8 | convolution fusion | flops 2152726528 | bytes 15204352 | tf_op jit(solution)/shard_map/dot_general | solution.py:52
  16.9 3.4 fusion.37
  20.9 1.5 multiply_reduce_fusion.12
  22.3 1.4 multiply_convert_fusion.11.refs_5_.refs_12_
  23.8 6.4 %fusion.41.refs_1_ = f32[256,3072]{1,0:T(8,128)} fusion(bf16[256,1024]{1,0:T(8,128)(2,1)S(1)} %multiply_convert_fusion.11.refs_5_.refs_12_, bf16[1024,3072]{1,0:T(8,128)(2,1)} %param.29), kind=kOutput, calls=%fused_computation.152 | convolution fusion | flops 1610612736 | bytes 9961472 | tf_op jit(solution)/shard_map/dot_general | solution.py:1284
  31.5 1.9 copy-done.8
  33.4 32.6 %shard_map.323 = (bf16[1024,768]{1,0:T(8,128)(2,1)S(1)}, bf16[256,1024]{1,0:T(8,128)(2,1)S(1)}, bf16[256,1024]{1,0:T(8,128)(2,1)S(1)}, bf16[256,1024]{1,0:T(8,128)(2,1)S(1)}) custom-call(s32[1]{0:T(128)} %dynamic_slice.3.refs_0_.length_ref, f32[256,3072]{1,0:T(8,128)S(1)} %copy-done.8, f32[3,256,128]{2,1,0:T(8,128)S(1)} %pad_maximum_fusion.3.refs_2_, ...), custom_call_target="tpu_custom_call" | custom-call | flops 1073741824 | bytes 5242880 | tf_op jit(solution)/shard_map/pallas_call | solution.py:616
  68.1 1.6 copy-done.39
  69.7 1.3 fusion.42
  72.1 17.3 %shard_map.324 = (f32[256,1024]{1,0:T(8,128)S(1)}, f32[272,1024]{1,0:T(8,128)S(1)}, f32[2,1024]{1,0:T(2,128)S(1)}) custom-call(s32[1]{0:T(128)} %dynamic_slice.3.refs_0_.length_ref, bf16[256,1024]{1,0:T(8,128)(2,1)S(1)} %multiply_convert_fusion.9.glu_ref, f32[5,1024]{1,0:T(8,128)S(1)} %convert_element_type.167.kernel_ref), custom_call_target="tpu_custom_call" | custom-call | tf_op jit(solution)/shard_map/pallas_call | solution.py:238
  92.2 2.2 fusion.39
  94.9 8.1 %multiply_convert_fusion = (bf16[256,4096]{1,0:T(8,128)(2,1)S(1)}, f32[256,4096]{1,0:T(8,128)}) fusion(bf16[256,1024]{1,0:T(8,128)(2,1)S(1)} %multiply_convert_fusion.7.refs_5_.refs_0_, bf16[1024,4096]{1,0:T(8,128)(2,1)} %param.36), kind=kOutput, calls=%fused_computation.6 | convolution fusion | flops 2152726528 | bytes 15204352 | tf_op jit(solution)/shard_map/dot_general | solution.py:52
  103.0 2.5 fusion.40
  106.3 1.2 fusion.33
  107.7 5.5 %fusion.3.refs_6_.refs_1_ = bf16[256,4096]{1,0:T(8,128)(2,1)S(1)} fusion(bf16[256,1024]{1,0:T(8,128)(2,1)S(1)} %multiply_convert_fusion.5.refs_4_, bf16[4096,1024]{1,0:T(8,128)(2,1)S(1)} %bitcast.133, f32[256,4096]{1,0:T(8,128)} %get-tuple-element.142), kind=kOutput, calls=%fused_computation.5 | convolution fusion | flops 2156920832 | bytes 15204352 | tf_op jit(solution)/shard_map/dot_general | solution.py:44
  113.2 15.5 %multiply_reduce_fusion.1 = (f32[1024]{0:T(1024)S(1)}, f32[256]{0:T(256)S(1)}, f32[256,1024]{1,0:T(8,128)S(1)}) fusion(f32[256,1024]{1,0:T(8,128)S(1)} %get-tuple-element.140, f32[256]{0:T(256)S(1)} %fusion.25, f32[256]{0:T(256)S(1)} %broadcast_multiply_fusion.5, f32[1024]{0:T(1024)S(1)} %bitcast.115, bf16[256,4096]{1,0:T(8,128)(2,1)S(1)} %fusion.3.refs_6_.refs_1_, ...), kind=kOutput, calls=%fused_computation.38 | convolution fusion | flops 2149317376 | bytes 12594176 | tf_op jit(solution)/shard_map/dot_general | solution.py:44
  130.8 14.8 %shard_map.325 = (f32[256,1024]{1,0:T(8,128)S(1)}, f32[8,1024]{1,0:T(8,128)S(1)}, f32[2,1024]{1,0:T(2,128)S(1)}) custom-call(s32[1]{0:T(128)} %dynamic_slice.3.refs_0_.length_ref, f32[1]{0:T(128)} %bitcast.20.count_ref, f32[256,1024]{1,0:T(8,128)S(1)} %fusion.4.grad_ref, f32[256,1024]{1,0:T(8,128)S(1)} %get-tuple-element.48.conv_ref, ...), custom_call_target="tpu_custom_call" | custom-call | tf_op jit(solution)/shard_map/pallas_call | solution.py:349
  146.2 1.5 multiply_reduce_fusion.2
  150.2 1.9 multiply_sine_fusion
  153.0 47.4 %shard_map.326 = (bf16[256,3072]{1,0:T(8,128)(2,1)S(1)}, bf16[256,1024]{1,0:T(8,128)(2,1)S(1)}, bf16[3,256,1024]{2,1,0:T(8,128)(2,1)S(1)}) custom-call(s32[1]{0:T(128)} %dynamic_slice.3.refs_0_.length_ref, bf16[1024,768]{1,0:T(8,128)(2,1)S(1)} %copy-done.12, bf16[256,1024]{1,0:T(8,128)(2,1)S(1)} %convolution_convert_fusion.refs_2_, ...), custom_call_target="tpu_custom_call" | custom-call | flops 2684354560 | bytes 4194304 | tf_op jit(solution)/shard_map/pallas_call | solution.py:795
  200.5 2.3 multiply_reduce_fusion.3
  204.0 1.4 slice-done.5
  205.4 1.4 copy-done.45
  206.9 3.1 fusion.2.refs_18_
  210.0 6.8 %multiply_reduce_fusion.4 = (f32[1024]{0:T(1024)S(1)}, f32[256]{0:T(256)S(1)}, f32[256,1024]{1,0:T(8,128)S(1)}) fusion(bf16[1,256,1024]{2,1,0:T(8,128)(2,1)S(1)} %copy-done.22, f32[256]{0:T(256)S(1)} %fusion.22, f32[256]{0:T(256)S(1)} %broadcast_multiply_fusion.8, f32[1024]{0:T(1024)S(1)} %bitcast.94, f32[256]{0:T(256)S(1)} %bitcast.102, ...), kind=kOutput, calls=%fused_computation.41 | convolution fusion | flops 2150365952 | bytes 12079104 | tf_op jit(solution)/shard_map/dot_general | solution.py:44
  220.5 154.4 %shard_map.327 = (f32[256,512]{1,0:T(8,128)}, f32[128,1024]{1,0:T(8,128)}, f32[256,256]{1,0:T(8,128)}, f32[256,128]{1,0:T(8,128)}, f32[256,128]{1,0:T(8,128)}, /...) custom-call(bf16[256,1024]{1,0:T(8,128)(2,1)} %copy-done.7, ...), custom_call_target="tpu_custom_call" | custom-call | flops 12348030976 | bytes 419430400 | tf_op jit(solution)/shard_map/pallas_call | solution.py:1209
  374.9 1.3 slice.75
  376.2 1.3 fusion.34
  377.5 4.2 %shard_map.328 = (f32[256,512]{1,0:T(8,128)}, f32[128,1024]{1,0:T(8,128)}, f32[256,256]{1,0:T(8,128)}, f32[256,128]{1,0:T(8,128)}, f32[256,128]{1,0:T(8,128)}, /...) custom-call(f32[256,512]{1,0:T(8,128)} %get-tuple-element.60.refs_0_, ...), custom_call_target="tpu_custom_call" | custom-call | tf_op jit(solution)/shard_map/pallas_call | solution.py:1225
  (188 shorter events, 23.8 us)
Async XLA Ops:
  0.7 91.5 %copy-start = (bf16[1024,1024]{1,0:T(8,128)(2,1)S(1)}, bf16[1024,1024]{1,0:T(8,128)(2,1)}, u32[]{:S(2)}) copy-start(bf16[1024,1024]{1,0:T(8,128)(2,1)} %param.35) | copy-start | bytes 6291460
  7.3 9.6 %slice-start.2 = ((s8[8388608]{0:T(1024)(128)(4,1)}), s8[4194304]{0:T(1024)(128)(4,1)S(1)}, s32[]{:S(2)}) async-start(s8[8388608]{0:T(1024)(128)(4,1)} %bitcast.134), calls=%async_computation.2 | async-start | bytes 8388608
  8.8 22.6 %copy-start.5 = (bf16[256,1024]{1,0:T(8,128)(2,1)}, bf16[256,1024]{1,0:T(8,128)(2,1)S(1)}, u32[]{:S(2)}) copy-start(bf16[256,1024]{1,0:T(8,128)(2,1)S(1)} %multiply_convert_fusion.12.refs_4_.refs_17_) | copy-start | bytes 1572868
  8.8 8.0 %copy-start.21 = (bf16[1,256,1024]{2,1,0:T(8,128)(2,1)S(1)}, bf16[1,256,1024]{2,1,0:T(8,128)(2,1)}, u32[]{:S(2)}) copy-start(bf16[1,256,1024]{2,1,0:T(8,128)(2,1)} %param.20) | copy-start | bytes 1572868
  8.9 8.0 %slice-start.3 = ((s8[8388608]{0:T(1024)(128)(4,1)}), s8[4194304]{0:T(1024)(128)(4,1)S(1)}, s32[]{:S(2)}) async-start(s8[8388608]{0:T(1024)(128)(4,1)} %bitcast.134), calls=%async_computation.3 | async-start | bytes 8388608
  23.8 7.7 %copy-start.6 = (bf16[256,1024]{1,0:T(8,128)(2,1)}, bf16[256,1024]{1,0:T(8,128)(2,1)S(1)}, u32[]{:S(2)}) copy-start(bf16[256,1024]{1,0:T(8,128)(2,1)S(1)} %multiply_convert_fusion.11.refs_5_.refs_12_) | copy-start | bytes 1572868
  33.4 32.7 %copy-start.19 = (f32[256,1024]{1,0:T(8,128)S(1)}, f32[256,1024]{1,0:T(8,128)}, u32[]{:S(2)}) copy-start(f32[256,1024]{1,0:T(8,128)} %get-tuple-element.136) | copy-start | bytes 3145732
  33.4 32.7 %copy-start.26 = (bf16[1024,1024]{1,0:T(8,128)(2,1)S(1)}, bf16[1024,1024]{1,0:T(8,128)(2,1)}, u32[]{:S(2)}) copy-start(bf16[1024,1024]{1,0:T(8,128)(2,1)} %param.30) | copy-start | bytes 6291460
  66.0 5.0 %copy-start.4 = (bf16[256,1024]{1,0:T(8,128)(2,1)}, bf16[256,1024]{1,0:T(8,128)(2,1)S(1)}, u32[]{:S(2)}) copy-start(bf16[256,1024]{1,0:T(8,128)(2,1)S(1)} %get-tuple-element.47.refs_8_) | copy-start | bytes 1572868
  66.0 5.0 %copy-start.11 = (bf16[1024,768]{1,0:T(8,128)(2,1)}, bf16[1024,768]{1,0:T(8,128)(2,1)S(1)}, u32[]{:S(2)}) copy-start(bf16[1024,768]{1,0:T(8,128)(2,1)S(1)} %get-tuple-element.52.refs_1_) | copy-start | bytes 4718596
  66.0 5.0 %copy-start.14 = (bf16[256,1024]{1,0:T(8,128)(2,1)}, bf16[256,1024]{1,0:T(8,128)(2,1)S(1)}, u32[]{:S(2)}) copy-start(bf16[256,1024]{1,0:T(8,128)(2,1)S(1)} %get-tuple-element.57.refs_19_) | copy-start | bytes 1572868
  66.0 5.0 %copy-start.15 = (bf16[256,1024]{1,0:T(8,128)(2,1)}, bf16[256,1024]{1,0:T(8,128)(2,1)S(1)}, u32[]{:S(2)}) copy-start(bf16[256,1024]{1,0:T(8,128)(2,1)S(1)} %get-tuple-element.56.refs_14_) | copy-start | bytes 1572868
  69.7 20.7 %copy-start.37 = (bf16[1024]{0:T(1024)(128)(2,1)S(1)}, bf16[1024]{0:T(1024)(128)(2,1)}, u32[]{:S(2)}) copy-start(bf16[1024]{0:T(1024)(128)(2,1)} %param.34) | copy-start | bytes 6148
  69.7 20.7 %copy-start.38 = (bf16[1024]{0:T(1024)(128)(2,1)S(1)}, bf16[1024]{0:T(1024)(128)(2,1)}, u32[]{:S(2)}) copy-start(bf16[1024]{0:T(1024)(128)(2,1)} %param.33) | copy-start | bytes 6148
  71.1 18.4 %copy-start.23 = (f32[256,2048]{1,0:T(8,128)}, f32[256,2048]{1,0:T(8,128)S(1)}, u32[]{:S(2)}) copy-start(f32[256,2048]{1,0:T(8,128)S(1)} %fusion.42) | copy-start | bytes 6291460
  92.2 10.9 %copy-start.25 = (bf16[256,1024]{1,0:T(8,128)(2,1)}, bf16[256,1024]{1,0:T(8,128)(2,1)S(1)}, u32[]{:S(2)}) copy-start(bf16[256,1024]{1,0:T(8,128)(2,1)S(1)} %multiply_convert_fusion.8.refs_10_) | copy-start | bytes 1572868
  94.7 8.4 %slice-start = ((s8[8388608]{0:T(1024)(128)(4,1)}), s8[4194304]{0:T(1024)(128)(4,1)S(1)}, s32[]{:S(2)}) async-start(s8[8388608]{0:T(1024)(128)(4,1)} %bitcast.132), calls=%async_computation | async-start | bytes 8388608
  94.9 58.1 %copy-start.7 = (bf16[256,1024]{1,0:T(8,128)(2,1)}, bf16[256,1024]{1,0:T(8,128)(2,1)S(1)}, u32[]{:S(2)}) copy-start(bf16[256,1024]{1,0:T(8,128)(2,1)S(1)} %multiply_convert_fusion.7.refs_5_.refs_0_) | copy-start | bytes 1572868
  94.9 8.1 %slice-start.1 = ((s8[8388608]{0:T(1024)(128)(4,1)}), s8[4194304]{0:T(1024)(128)(4,1)S(1)}, s32[]{:S(2)}) async-start(s8[8388608]{0:T(1024)(128)(4,1)} %bitcast.132), calls=%async_computation.1 | async-start | bytes 8388608
  107.7 5.5 %copy-start.33 = (bf16[256,1024]{1,0:T(8,128)(2,1)}, bf16[256,1024]{1,0:T(8,128)(2,1)S(1)}, u32[]{:S(2)}) copy-start(bf16[256,1024]{1,0:T(8,128)(2,1)S(1)} %multiply_convert_fusion.5.refs_4_) | copy-start | bytes 1572868
  113.2 39.8 %copy-start.10 = (bf16[256,4096]{1,0:T(8,128)(2,1)}, bf16[256,4096]{1,0:T(8,128)(2,1)S(1)}, u32[]{:S(2)}) copy-start(bf16[256,4096]{1,0:T(8,128)(2,1)S(1)} %fusion.3.refs_6_.refs_1_) | copy-start | bytes 6291460
  129.4 16.2 %copy-start.24 = (f32[256,2048]{1,0:T(8,128)S(1)}, f32[256,2048]{1,0:T(8,128)}, u32[]{:S(2)}) copy-start(f32[256,2048]{1,0:T(8,128)} %copy-done.23) | copy-start | bytes 6291460
  130.4 15.8 %copy-start.18 = (f32[256,1024]{1,0:T(8,128)S(1)}, f32[256,1024]{1,0:T(8,128)}, u32[]{:S(2)}) copy-start(f32[256,1024]{1,0:T(8,128)} %copy-done.17) | copy-start | bytes 3145732
  130.5 15.8 %copy-start.40 = (bf16[1024,2048]{1,0:T(8,128)(2,1)S(1)}, bf16[1024,2048]{1,0:T(8,128)(2,1)}, u32[]{:S(2)}) copy-start(bf16[1024,2048]{1,0:T(8,128)(2,1)} %param.31) | copy-start | bytes 12582916
  152.4 48.1 %slice-start.6 = ((s8[6291456]{0:T(1024)(128)(4,1)}), s8[4194304]{0:T(1024)(128)(4,1)S(1)}, s32[]{:S(2)}) async-start(s8[6291456]{0:T(1024)(128)(4,1)} %bitcast.138), calls=%async_computation.6 | async-start | bytes 8388608
  153.0 47.5 %copy-start.20 = (f32[256,1024]{1,0:T(8,128)S(1)}, f32[256,1024]{1,0:T(8,128)}, u32[]{:S(2)}) copy-start(f32[256,1024]{1,0:T(8,128)} %get-tuple-element.136) | copy-start | bytes 3145732
  153.0 47.5 %slice-start.7 = ((s8[6291456]{0:T(1024)(128)(4,1)}), s8[2097152]{0:T(1024)(128)(4,1)S(1)}, s32[]{:S(2)}) async-start(s8[6291456]{0:T(1024)(128)(4,1)} %bitcast.138), calls=%async_computation.7 | async-start | bytes 4194304
  203.6 6.4 %copy-start.31 = (bf16[256,1024]{1,0:T(8,128)(2,1)}, bf16[256,1024]{1,0:T(8,128)(2,1)S(1)}, u32[]{:S(2)}) copy-start(bf16[256,1024]{1,0:T(8,128)(2,1)S(1)} %get-tuple-element.95.refs_15_) | copy-start | bytes 1572868
  210.0 6.8 %copy-start.42 = (bf16[256,4096]{1,0:T(8,128)(2,1)}, bf16[256,4096]{1,0:T(8,128)(2,1)S(1)}, u32[]{:S(2)}) copy-start(bf16[256,4096]{1,0:T(8,128)(2,1)S(1)} %fusion.2.refs_18_) | copy-start | bytes 6291460
  220.5 161.9 %copy-start.35 = (f32[1024]{0:T(1024)S(1)}, f32[1024]{0:T(1024)}, u32[]{:S(2)}) copy-start(f32[1024]{0:T(1024)} %param.38) | copy-start | bytes 12292
  220.5 162.5 %copy-start.36 = (f32[1024]{0:T(1024)S(1)}, f32[1024]{0:T(1024)}, u32[]{:S(2)}) copy-start(f32[1024]{0:T(1024)} %param.39) | copy-start | bytes 12292
  220.5 163.1 %copy-start.1 = (bf16[1024,1024]{1,0:T(8,128)(2,1)S(1)}, bf16[1024,1024]{1,0:T(8,128)(2,1)}, u32[]{:S(2)}) copy-start(bf16[1024,1024]{1,0:T(8,128)(2,1)} %param.35) | copy-start | bytes 6291460
  (22 other events, 57.3 us)

commit v2 on v1

--- a/solution.py
+++ b/solution.py
@@ -1174,12 +1174,17 @@
             lax.fori_loop(0, 1 << level, one_wait, 0)
 
 
-def pass_kernel(count, *refs):
-    for source, target in zip(refs[:count], refs[count:]):
+def pass_kernel(count, cuts, *refs):
+    sources, share, targets, pieces = refs[:count], refs[count], refs[count + 1 : -len(cuts)], refs[-len(cuts) :]
+    for source, target in zip(sources, targets):
         target[...] = source[...]
-
-
-def scatter_sums(jobs, sequence, rows, collective_id):
+    start = 0
+    for cut, piece in zip(cuts, pieces):
+        piece[...] = share[start : start + cut, :]
+        start += cut
+
+
+def scatter_sums(jobs, sequence, rows, cuts, collective_id):
     height, width = rows.shape
     width = width // jobs[0].groups
     if width % 128 or not all(job.fits() for job in jobs):
@@ -1192,7 +1197,8 @@
             ]
             for job in jobs
         ]
-        return sums, share
+        starts = [sum(cuts[:i]) for i in range(len(cuts))]
+        return sums, [share[start : start + cut] for start, cut in zip(starts, cuts)]
     scratch, operands, outs = [], [], []
     for job in jobs:
         block = (job.rows, job.cols)
@@ -1219,19 +1225,22 @@
             flops=sum(job.flops() for job in jobs), bytes_accessed=400 << 20, transcendentals=0
         ),
     )(*operands, rows)
-    passes = 4
+    passes = 2
     specs = [pl.BlockSpec((out.shape[0] // passes, out.shape[1]), lambda i: (i, 0)) for out in outs]
+    whole_specs = [pl.BlockSpec((rows, width), lambda i: (0, 0)) for rows in (height, *cuts)]
+    pieces = [jax.ShapeDtypeStruct((cut, width), jnp.float32) for cut in cuts]
     results = list(
         pl.pallas_call(
-            functools.partial(pass_kernel, len(outs)),
-            out_shape=outs,
+            functools.partial(pass_kernel, len(outs), cuts),
+            out_shape=[*outs, *pieces],
             grid=(passes,),
-            in_specs=specs,
-            out_specs=specs,
+            in_specs=[*specs, whole_specs[0]],
+            out_specs=[*specs, *whole_specs[1:]],
             compiler_params=pltpu.CompilerParams(vmem_limit_bytes=60 << 20),
-        )(*results)
-    )
-    return [[results.pop(0) for _ in job.parts] for job in jobs], share
+        )(*results, share)
+    )
+    sums = [[results.pop(0) for _ in job.parts] for job in jobs]
+    return sums, results
 
 
 def shards(
@@ -1265,15 +1274,14 @@
     item_index = lax.axis_index("batch")
     seq_length = frames * groups
     level_count = cond_table.shape[0] - 1
-    cond_rows = cond_table.astype(jnp.float32)
-    gain_rows = norm_gains.astype(jnp.float32)
+    gain_rows = [norm_gains[row].astype(jnp.float32) for row in range(norm_gains.shape[0])]
     level_hot = (jnp.arange(level_count) == levels[0] - 1).astype(jnp.float32)
-    level_vector = jnp.sum(level_hot[:, None] * cond_rows[:level_count], axis=0)
+    level_vector = lax.dynamic_slice_in_dim(cond_table, levels[0] - 1, 1)[0].astype(jnp.float32)
     mask_column = token_mask[0].astype(jnp.float32)[:, None]
     start_rows = (
         frames_in[0].astype(jnp.float32)
         + level_vector[None, :]
-        + mask_column * cond_rows[level_count][None, :]
+        + mask_column * cond_table[level_count].astype(jnp.float32)[None, :]
     )
     length = lax.dynamic_slice_in_dim(lengths, item_index, 1)[0]
     positions = seq_index * frames + jnp.arange(frames)
@@ -1372,21 +1380,21 @@
         Job([ffn1_down_pair[::-1]], True, "xy12"),
         Job([ffn1_up_pair], False, "12xy", far_ffn1),
     ]
-    sums, small_piece = scatter_sums(jobs, SEGMENTS, small_rows, 7)
-    cond_end = 5 + level_count + 1
+    cuts = (5, level_count + 1, taps)
+    sums, (gain_sums, cond_sums, tap_sums) = scatter_sums(jobs, SEGMENTS, small_rows, cuts, 7)
     new_mean = 0.9 * running_mean + 0.1 * batchnorm_frame_mean
     new_var = 0.9 * running_var + 0.1 * bn_var * count_of_frames / (count_of_frames - 1.0)
     return (
         out_rows[None],
         grad_zero.astype(jnp.bfloat16)[None],
-        small_piece[5:cond_end],
-        small_piece[0:5],
+        cond_sums,
+        gain_sums,
         sums[5][0],
         sums[4][0],
         sums[3][0],
         sums[2][1],
         sums[2][0],
-        small_piece[cond_end : cond_end + taps],
+        tap_sums,
         gradient_normalized_sum,
         gradient_sum_total,
         sums[2][2],

time: 388 us -> 383 us (0.987)
  local copies, waits for them, and re-layouts: 16.6 us -> 12.2 us
    slice x4 -> x0, local copies, waits for them, and re-layouts: 4.34 us -> none  [the longest x1 1.35 us: shards(): small_piece[5:cond_end]]
where the time goes in v2:
time: 383 us; the launch traced here: 379 us
  Pallas kernels  270 us (70%)
  matrix products  69.1 us (18%)
  other arithmetic  25 us (7%)
  local copies, waits for them, and re-layouts  12.2 us (3%)
    pallas_call x1, Pallas kernels, scatter_sums(): pl.pallas_call(functools.partial(scatter_kernel, jobs, sequence), out_sha...  154 us
    pallas_call x1, Pallas kernels, attend_back(): pl.pallas_call(functools.partial(attend_back_kernel, groups, heads, side)...  47.4 us
    dot_general x8, matrix products, times_transposed(): lax.dot_general(left_side, weight, (((1,), (1,)), ((), ())), preferred_el...  36.4 us
    pallas_call x1, Pallas kernels, attend(): pl.pallas_call(functools.partial(attend_kernel, groups, heads, side), out...  32.6 us
    pallas_call x1, Pallas kernels, convolve(): pl.pallas_call(functools.partial(convolve_kernel, groups, batches, taps),...  17.3 us
    dot_general x2, matrix products, ffn_forward(): hidden = jnp.dot(lowered, up_weight, preferred_element_type=jnp.float32)  16.1 us
    pallas_call x1, Pallas kernels, convolve_back(): pl.pallas_call(functools.partial(convolve_back_kernel, groups, batches, t...  14.8 us
    unnamed x108, local copies, waits for them, and re-layouts  10.1 us

profile of v2, /device:TPU:0, one launch (start us, length us, event | category | flops | bytes accessed | tf_op | source)
XLA Modules:
  0.0 379.2 jit_solution(16341727639751917752)
XLA Ops:
  3.8 1.3 fusion.16
  5.1 1.4 multiply_reduce_fusion.13
  6.5 1.5 multiply_convert_fusion.12.refs_4_.refs_17_
  8.1 8.0 %multiply_convert_fusion.1 = (bf16[256,4096]{1,0:T(8,128)(2,1)S(1)}, f32[256,4096]{1,0:T(8,128)}) fusion(bf16[256,1024]{1,0:T(8,128)(2,1)S(1)} %multiply_convert_fusion.12.refs_4_.refs_17_, bf16[1024,4096]{1,0:T(8,128)(2,1)} %param.27), kind=kOutput, calls=%fused_computation.8 | convolution fusion | flops 2152726528 | bytes 15204352 | tf_op jit(solution)/shard_map/dot_general | solution.py:52
  16.1 3.4 fusion.34
  20.1 1.5 multiply_reduce_fusion.12
  21.6 1.4 multiply_convert_fusion.11.refs_5_.refs_12_
  23.0 6.5 %fusion.38.refs_1_ = f32[256,3072]{1,0:T(8,128)} fusion(bf16[256,1024]{1,0:T(8,128)(2,1)S(1)} %multiply_convert_fusion.11.refs_5_.refs_12_, bf16[1024,3072]{1,0:T(8,128)(2,1)} %param.29), kind=kOutput, calls=%fused_computation.155 | convolution fusion | flops 1610612736 | bytes 9961472 | tf_op jit(solution)/shard_map/dot_general | solution.py:1292
  30.7 1.9 copy-done.8
  32.6 32.6 %shard_map.323 = (bf16[1024,768]{1,0:T(8,128)(2,1)S(1)}, bf16[256,1024]{1,0:T(8,128)(2,1)S(1)}, bf16[256,1024]{1,0:T(8,128)(2,1)S(1)}, bf16[256,1024]{1,0:T(8,128)(2,1)S(1)}) custom-call(s32[1]{0:T(128)} %dynamic_slice.7.refs_0_.length_ref, f32[256,3072]{1,0:T(8,128)S(1)} %copy-done.8, f32[3,256,128]{2,1,0:T(8,128)S(1)} %pad_maximum_fusion.3.refs_2_, ...), custom_call_target="tpu_custom_call" | custom-call | flops 1073741824 | bytes 5242880 | tf_op jit(solution)/shard_map/pallas_call | solution.py:616
  67.3 1.6 copy-done.39
  69.0 1.3 fusion.39
  71.3 17.3 %shard_map.324 = (f32[256,1024]{1,0:T(8,128)S(1)}, f32[272,1024]{1,0:T(8,128)S(1)}, f32[2,1024]{1,0:T(2,128)S(1)}) custom-call(s32[1]{0:T(128)} %dynamic_slice.7.refs_0_.length_ref, bf16[256,1024]{1,0:T(8,128)(2,1)S(1)} %multiply_convert_fusion.9.glu_ref, f32[5,1024]{1,0:T(8,128)S(1)} %convert_element_type.172.kernel_ref), custom_call_target="tpu_custom_call" | custom-call | tf_op jit(solution)/shard_map/pallas_call | solution.py:238
  91.3 2.2 fusion.36
  94.1 8.1 %multiply_convert_fusion = (bf16[256,4096]{1,0:T(8,128)(2,1)S(1)}, f32[256,4096]{1,0:T(8,128)}) fusion(bf16[256,1024]{1,0:T(8,128)(2,1)S(1)} %multiply_convert_fusion.7.refs_5_.refs_0_, bf16[1024,4096]{1,0:T(8,128)(2,1)} %param.36), kind=kOutput, calls=%fused_computation.6 | convolution fusion | flops 2152726528 | bytes 15204352 | tf_op jit(solution)/shard_map/dot_general | solution.py:52
  102.2 2.5 fusion.37
  105.5 1.2 fusion.32
  106.9 5.5 %fusion.3.refs_6_.refs_1_ = bf16[256,4096]{1,0:T(8,128)(2,1)S(1)} fusion(bf16[256,1024]{1,0:T(8,128)(2,1)S(1)} %multiply_convert_fusion.5.refs_4_, bf16[4096,1024]{1,0:T(8,128)(2,1)S(1)} %bitcast.141, f32[256,4096]{1,0:T(8,128)} %get-tuple-element.148), kind=kOutput, calls=%fused_computation.5 | convolution fusion | flops 2156920832 | bytes 15204352 | tf_op jit(solution)/shard_map/dot_general | solution.py:44
  112.3 15.5 %multiply_reduce_fusion.1 = (f32[1024]{0:T(1024)S(1)}, f32[256]{0:T(256)S(1)}, f32[256,1024]{1,0:T(8,128)S(1)}) fusion(f32[256,1024]{1,0:T(8,128)S(1)} %get-tuple-element.146, f32[256]{0:T(256)S(1)} %fusion.24, f32[256]{0:T(256)S(1)} %broadcast_multiply_fusion.5, f32[1024]{0:T(1024)S(1)} %bitcast.123, bf16[256,4096]{1,0:T(8,128)(2,1)S(1)} %fusion.3.refs_6_.refs_1_, ...), kind=kOutput, calls=%fused_computation.38 | convolution fusion | flops 2149317376 | bytes 12594176 | tf_op jit(solution)/shard_map/dot_general | solution.py:44
  130.0 14.8 %shard_map.325 = (f32[256,1024]{1,0:T(8,128)S(1)}, f32[8,1024]{1,0:T(8,128)S(1)}, f32[2,1024]{1,0:T(2,128)S(1)}) custom-call(s32[1]{0:T(128)} %dynamic_slice.7.refs_0_.length_ref, f32[1]{0:T(128)} %bitcast.22.count_ref, f32[256,1024]{1,0:T(8,128)S(1)} %fusion.4.grad_ref, f32[256,1024]{1,0:T(8,128)S(1)} %get-tuple-element.51.conv_ref, ...), custom_call_target="tpu_custom_call" | custom-call | tf_op jit(solution)/shard_map/pallas_call | solution.py:349
  145.4 1.5 multiply_reduce_fusion.2
  149.3 1.9 multiply_sine_fusion
  152.2 47.4 %shard_map.326 = (bf16[256,3072]{1,0:T(8,128)(2,1)S(1)}, bf16[256,1024]{1,0:T(8,128)(2,1)S(1)}, bf16[3,256,1024]{2,1,0:T(8,128)(2,1)S(1)}) custom-call(s32[1]{0:T(128)} %dynamic_slice.7.refs_0_.length_ref, bf16[1024,768]{1,0:T(8,128)(2,1)S(1)} %copy-done.12, bf16[256,1024]{1,0:T(8,128)(2,1)S(1)} %convolution_convert_fusion.refs_2_, ...), custom_call_target="tpu_custom_call" | custom-call | flops 2684354560 | bytes 4194304 | tf_op jit(solution)/shard_map/pallas_call | solution.py:795
  199.7 2.3 multiply_reduce_fusion.3
  203.2 1.4 slice-done.5
  204.6 1.4 copy-done.45
  206.1 3.0 fusion.2.refs_18_
  209.1 6.8 %multiply_reduce_fusion.4 = (f32[1024]{0:T(1024)S(1)}, f32[256]{0:T(256)S(1)}, f32[256,1024]{1,0:T(8,128)S(1)}) fusion(bf16[1,256,1024]{2,1,0:T(8,128)(2,1)S(1)} %copy-done.22, f32[256]{0:T(256)S(1)} %fusion.21, f32[256]{0:T(256)S(1)} %broadcast_multiply_fusion.8, f32[1024]{0:T(1024)S(1)} %bitcast.102, f32[256]{0:T(256)S(1)} %bitcast.110, ...), kind=kOutput, calls=%fused_computation.41 | convolution fusion | flops 2150365952 | bytes 12079104 | tf_op jit(solution)/shard_map/dot_general | solution.py:44
  216.6 1.1 multiply_reduce_fusion
  217.6 1.1 pad_maximum_fusion.refs_7_
  219.6 154.4 %shard_map.327 = (f32[256,512]{1,0:T(8,128)}, f32[128,1024]{1,0:T(8,128)}, f32[256,256]{1,0:T(8,128)}, f32[256,128]{1,0:T(8,128)}, f32[256,128]{1,0:T(8,128)}, /...) custom-call(bf16[256,1024]{1,0:T(8,128)(2,1)} %copy-done.7, ...), custom_call_target="tpu_custom_call" | custom-call | flops 12348030976 | bytes 419430400 | tf_op jit(solution)/shard_map/pallas_call | solution.py:1215
  374.0 3.2 shard_map.328
  (184 shorter events, 21.0 us)
Async XLA Ops:
  0.7 90.7 %copy-start = (bf16[1024,1024]{1,0:T(8,128)(2,1)S(1)}, bf16[1024,1024]{1,0:T(8,128)(2,1)}, u32[]{:S(2)}) copy-start(bf16[1024,1024]{1,0:T(8,128)(2,1)} %param.35) | copy-start | bytes 6291460
  6.5 9.6 %slice-start.2 = ((s8[8388608]{0:T(1024)(128)(4,1)}), s8[4194304]{0:T(1024)(128)(4,1)S(1)}, s32[]{:S(2)}) async-start(s8[8388608]{0:T(1024)(128)(4,1)} %bitcast.142), calls=%async_computation.2 | async-start | bytes 8388608
  8.1 22.6 %copy-start.5 = (bf16[256,1024]{1,0:T(8,128)(2,1)}, bf16[256,1024]{1,0:T(8,128)(2,1)S(1)}, u32[]{:S(2)}) copy-start(bf16[256,1024]{1,0:T(8,128)(2,1)S(1)} %multiply_convert_fusion.12.refs_4_.refs_17_) | copy-start | bytes 1572868
  8.1 8.0 %copy-start.21 = (bf16[1,256,1024]{2,1,0:T(8,128)(2,1)S(1)}, bf16[1,256,1024]{2,1,0:T(8,128)(2,1)}, u32[]{:S(2)}) copy-start(bf16[1,256,1024]{2,1,0:T(8,128)(2,1)} %param.20) | copy-start | bytes 1572868
  8.1 8.0 %slice-start.3 = ((s8[8388608]{0:T(1024)(128)(4,1)}), s8[4194304]{0:T(1024)(128)(4,1)S(1)}, s32[]{:S(2)}) async-start(s8[8388608]{0:T(1024)(128)(4,1)} %bitcast.142), calls=%async_computation.3 | async-start | bytes 8388608
  23.0 7.7 %copy-start.6 = (bf16[256,1024]{1,0:T(8,128)(2,1)}, bf16[256,1024]{1,0:T(8,128)(2,1)S(1)}, u32[]{:S(2)}) copy-start(bf16[256,1024]{1,0:T(8,128)(2,1)S(1)} %multiply_convert_fusion.11.refs_5_.refs_12_) | copy-start | bytes 1572868
  32.6 32.7 %copy-start.19 = (f32[256,1024]{1,0:T(8,128)S(1)}, f32[256,1024]{1,0:T(8,128)}, u32[]{:S(2)}) copy-start(f32[256,1024]{1,0:T(8,128)} %get-tuple-element.142) | copy-start | bytes 3145732
  32.6 32.7 %copy-start.26 = (bf16[1024,1024]{1,0:T(8,128)(2,1)S(1)}, bf16[1024,1024]{1,0:T(8,128)(2,1)}, u32[]{:S(2)}) copy-start(bf16[1024,1024]{1,0:T(8,128)(2,1)} %param.30) | copy-start | bytes 6291460
  65.3 5.0 %copy-start.4 = (bf16[256,1024]{1,0:T(8,128)(2,1)}, bf16[256,1024]{1,0:T(8,128)(2,1)S(1)}, u32[]{:S(2)}) copy-start(bf16[256,1024]{1,0:T(8,128)(2,1)S(1)} %get-tuple-element.50.refs_8_) | copy-start | bytes 1572868
  65.3 5.0 %copy-start.11 = (bf16[1024,768]{1,0:T(8,128)(2,1)}, bf16[1024,768]{1,0:T(8,128)(2,1)S(1)}, u32[]{:S(2)}) copy-start(bf16[1024,768]{1,0:T(8,128)(2,1)S(1)} %get-tuple-element.55.refs_1_) | copy-start | bytes 4718596
  65.3 5.0 %copy-start.14 = (bf16[256,1024]{1,0:T(8,128)(2,1)}, bf16[256,1024]{1,0:T(8,128)(2,1)S(1)}, u32[]{:S(2)}) copy-start(bf16[256,1024]{1,0:T(8,128)(2,1)S(1)} %get-tuple-element.60.refs_19_) | copy-start | bytes 1572868
  65.3 5.0 %copy-start.15 = (bf16[256,1024]{1,0:T(8,128)(2,1)}, bf16[256,1024]{1,0:T(8,128)(2,1)S(1)}, u32[]{:S(2)}) copy-start(bf16[256,1024]{1,0:T(8,128)(2,1)S(1)} %get-tuple-element.59.refs_14_) | copy-start | bytes 1572868
  69.0 20.7 %copy-start.37 = (bf16[1024]{0:T(1024)(128)(2,1)S(1)}, bf16[1024]{0:T(1024)(128)(2,1)}, u32[]{:S(2)}) copy-start(bf16[1024]{0:T(1024)(128)(2,1)} %param.34) | copy-start | bytes 6148
  69.0 20.7 %copy-start.38 = (bf16[1024]{0:T(1024)(128)(2,1)S(1)}, bf16[1024]{0:T(1024)(128)(2,1)}, u32[]{:S(2)}) copy-start(bf16[1024]{0:T(1024)(128)(2,1)} %param.33) | copy-start | bytes 6148
  70.3 18.3 %copy-start.23 = (f32[256,2048]{1,0:T(8,128)}, f32[256,2048]{1,0:T(8,128)S(1)}, u32[]{:S(2)}) copy-start(f32[256,2048]{1,0:T(8,128)S(1)} %fusion.39) | copy-start | bytes 6291460
  91.3 10.9 %copy-start.25 = (bf16[256,1024]{1,0:T(8,128)(2,1)}, bf16[256,1024]{1,0:T(8,128)(2,1)S(1)}, u32[]{:S(2)}) copy-start(bf16[256,1024]{1,0:T(8,128)(2,1)S(1)} %multiply_convert_fusion.8.refs_10_) | copy-start | bytes 1572868
  93.8 8.4 %slice-start = ((s8[8388608]{0:T(1024)(128)(4,1)}), s8[4194304]{0:T(1024)(128)(4,1)S(1)}, s32[]{:S(2)}) async-start(s8[8388608]{0:T(1024)(128)(4,1)} %bitcast.140), calls=%async_computation | async-start | bytes 8388608
  94.1 58.1 %copy-start.7 = (bf16[256,1024]{1,0:T(8,128)(2,1)}, bf16[256,1024]{1,0:T(8,128)(2,1)S(1)}, u32[]{:S(2)}) copy-start(bf16[256,1024]{1,0:T(8,128)(2,1)S(1)} %multiply_convert_fusion.7.refs_5_.refs_0_) | copy-start | bytes 1572868
  94.1 8.1 %slice-start.1 = ((s8[8388608]{0:T(1024)(128)(4,1)}), s8[4194304]{0:T(1024)(128)(4,1)S(1)}, s32[]{:S(2)}) async-start(s8[8388608]{0:T(1024)(128)(4,1)} %bitcast.140), calls=%async_computation.1 | async-start | bytes 8388608
  106.8 5.5 %copy-start.33 = (bf16[256,1024]{1,0:T(8,128)(2,1)}, bf16[256,1024]{1,0:T(8,128)(2,1)S(1)}, u32[]{:S(2)}) copy-start(bf16[256,1024]{1,0:T(8,128)(2,1)S(1)} %multiply_convert_fusion.5.refs_4_) | copy-start | bytes 1572868
  112.3 39.8 %copy-start.10 = (bf16[256,4096]{1,0:T(8,128)(2,1)}, bf16[256,4096]{1,0:T(8,128)(2,1)S(1)}, u32[]{:S(2)}) copy-start(bf16[256,4096]{1,0:T(8,128)(2,1)S(1)} %fusion.3.refs_6_.refs_1_) | copy-start | bytes 6291460
  128.5 16.3 %copy-start.24 = (f32[256,2048]{1,0:T(8,128)S(1)}, f32[256,2048]{1,0:T(8,128)}, u32[]{:S(2)}) copy-start(f32[256,2048]{1,0:T(8,128)} %copy-done.23) | copy-start | bytes 6291460
  129.6 15.8 %copy-start.18 = (f32[256,1024]{1,0:T(8,128)S(1)}, f32[256,1024]{1,0:T(8,128)}, u32[]{:S(2)}) copy-start(f32[256,1024]{1,0:T(8,128)} %copy-done.17) | copy-start | bytes 3145732
  129.6 15.8 %copy-start.40 = (bf16[1024,2048]{1,0:T(8,128)(2,1)S(1)}, bf16[1024,2048]{1,0:T(8,128)(2,1)}, u32[]{:S(2)}) copy-start(bf16[1024,2048]{1,0:T(8,128)(2,1)} %param.31) | copy-start | bytes 12582916
  151.6 48.1 %slice-start.6 = ((s8[6291456]{0:T(1024)(128)(4,1)}), s8[4194304]{0:T(1024)(128)(4,1)S(1)}, s32[]{:S(2)}) async-start(s8[6291456]{0:T(1024)(128)(4,1)} %bitcast.146), calls=%async_computation.6 | async-start | bytes 8388608
  152.2 47.5 %copy-start.20 = (f32[256,1024]{1,0:T(8,128)S(1)}, f32[256,1024]{1,0:T(8,128)}, u32[]{:S(2)}) copy-start(f32[256,1024]{1,0:T(8,128)} %get-tuple-element.142) | copy-start | bytes 3145732
  152.2 47.5 %slice-start.7 = ((s8[6291456]{0:T(1024)(128)(4,1)}), s8[2097152]{0:T(1024)(128)(4,1)S(1)}, s32[]{:S(2)}) async-start(s8[6291456]{0:T(1024)(128)(4,1)} %bitcast.146), calls=%async_computation.7 | async-start | bytes 4194304
  202.8 6.3 %copy-start.31 = (bf16[256,1024]{1,0:T(8,128)(2,1)}, bf16[256,1024]{1,0:T(8,128)(2,1)S(1)}, u32[]{:S(2)}) copy-start(bf16[256,1024]{1,0:T(8,128)(2,1)S(1)} %get-tuple-element.101.refs_15_) | copy-start | bytes 1572868
  209.1 6.8 %copy-start.42 = (bf16[256,4096]{1,0:T(8,128)(2,1)}, bf16[256,4096]{1,0:T(8,128)(2,1)S(1)}, u32[]{:S(2)}) copy-start(bf16[256,4096]{1,0:T(8,128)(2,1)S(1)} %fusion.2.refs_18_) | copy-start | bytes 6291460
  219.6 158.2 %copy-start.35 = (f32[1024]{0:T(1024)S(1)}, f32[1024]{0:T(1024)}, u32[]{:S(2)}) copy-start(f32[1024]{0:T(1024)} %param.38) | copy-start | bytes 12292
  219.6 158.8 %copy-start.36 = (f32[1024]{0:T(1024)S(1)}, f32[1024]{0:T(1024)}, u32[]{:S(2)}) copy-start(f32[1024]{0:T(1024)} %param.39) | copy-start | bytes 12292
  219.6 159.4 %copy-start.1 = (bf16[1024,1024]{1,0:T(8,128)(2,1)S(1)}, bf16[1024,1024]{1,0:T(8,128)(2,1)}, u32[]{:S(2)}) copy-start(bf16[1024,1024]{1,0:T(8,128)(2,1)} %param.35) | copy-start | bytes 6291460
  (22 other events, 57.2 us)

commit v3 on v2

--- a/solution.py
+++ b/solution.py
@@ -1225,7 +1225,7 @@
             flops=sum(job.flops() for job in jobs), bytes_accessed=400 << 20, transcendentals=0
         ),
     )(*operands, rows)
-    passes = 2
+    passes = 1
     specs = [pl.BlockSpec((out.shape[0] // passes, out.shape[1]), lambda i: (i, 0)) for out in outs]
     whole_specs = [pl.BlockSpec((rows, width), lambda i: (0, 0)) for rows in (height, *cuts)]
     pieces = [jax.ShapeDtypeStruct((cut, width), jnp.float32) for cut in cuts]

time: 383 us -> 383 us (level)
  no operation moved by 1% of the time
where the time goes in v3:
time: 383 us; the launch traced here: 379 us
  Pallas kernels  270 us (70%)
  matrix products  69.1 us (18%)
  other arithmetic  25 us (7%)
  local copies, waits for them, and re-layouts  12.2 us (3%)
    pallas_call x1, Pallas kernels, scatter_sums(): pl.pallas_call(functools.partial(scatter_kernel, jobs, sequence), out_sha...  154 us
    pallas_call x1, Pallas kernels, attend_back(): pl.pallas_call(functools.partial(attend_back_kernel, groups, heads, side)...  47.4 us
    dot_general x8, matrix products, times_transposed(): lax.dot_general(left_side, weight, (((1,), (1,)), ((), ())), preferred_el...  36.4 us
    pallas_call x1, Pallas kernels, attend(): pl.pallas_call(functools.partial(attend_kernel, groups, heads, side), out...  32.6 us
    pallas_call x1, Pallas kernels, convolve(): pl.pallas_call(functools.partial(convolve_kernel, groups, batches, taps),...  17.3 us
    dot_general x2, matrix products, ffn_forward(): hidden = jnp.dot(lowered, up_weight, preferred_element_type=jnp.float32)  16.1 us
    pallas_call x1, Pallas kernels, convolve_back(): pl.pallas_call(functools.partial(convolve_back_kernel, groups, batches, t...  14.8 us
    unnamed x108, local copies, waits for them, and re-layouts  10.1 us

profile of v3, /device:TPU:0, one launch (start us, length us, event | category | flops | bytes accessed | tf_op | source)
XLA Modules:
  0.0 379.5 jit_solution(11009926983988633060)
XLA Ops:
  3.8 1.3 fusion.16
  5.1 1.4 multiply_reduce_fusion.13
  6.5 1.5 multiply_convert_fusion.12.refs_4_.refs_17_
  8.1 8.0 %multiply_convert_fusion.1 = (bf16[256,4096]{1,0:T(8,128)(2,1)S(1)}, f32[256,4096]{1,0:T(8,128)}) fusion(bf16[256,1024]{1,0:T(8,128)(2,1)S(1)} %multiply_convert_fusion.12.refs_4_.refs_17_, bf16[1024,4096]{1,0:T(8,128)(2,1)} %param.27), kind=kOutput, calls=%fused_computation.8 | convolution fusion | flops 2152726528 | bytes 15204352 | tf_op jit(solution)/shard_map/dot_general | solution.py:52
  16.1 3.4 fusion.34
  20.1 1.5 multiply_reduce_fusion.12
  21.6 1.4 multiply_convert_fusion.11.refs_5_.refs_12_
  23.0 6.5 %fusion.38.refs_1_ = f32[256,3072]{1,0:T(8,128)} fusion(bf16[256,1024]{1,0:T(8,128)(2,1)S(1)} %multiply_convert_fusion.11.refs_5_.refs_12_, bf16[1024,3072]{1,0:T(8,128)(2,1)} %param.29), kind=kOutput, calls=%fused_computation.155 | convolution fusion | flops 1610612736 | bytes 9961472 | tf_op jit(solution)/shard_map/dot_general | solution.py:1292
  30.7 1.9 copy-done.8
  32.6 32.6 %shard_map.323 = (bf16[1024,768]{1,0:T(8,128)(2,1)S(1)}, bf16[256,1024]{1,0:T(8,128)(2,1)S(1)}, bf16[256,1024]{1,0:T(8,128)(2,1)S(1)}, bf16[256,1024]{1,0:T(8,128)(2,1)S(1)}) custom-call(s32[1]{0:T(128)} %dynamic_slice.7.refs_0_.length_ref, f32[256,3072]{1,0:T(8,128)S(1)} %copy-done.8, f32[3,256,128]{2,1,0:T(8,128)S(1)} %pad_maximum_fusion.3.refs_2_, ...), custom_call_target="tpu_custom_call" | custom-call | flops 1073741824 | bytes 5242880 | tf_op jit(solution)/shard_map/pallas_call | solution.py:616
  67.3 1.6 copy-done.39
  68.9 1.3 fusion.39
  71.3 17.3 %shard_map.324 = (f32[256,1024]{1,0:T(8,128)S(1)}, f32[272,1024]{1,0:T(8,128)S(1)}, f32[2,1024]{1,0:T(2,128)S(1)}) custom-call(s32[1]{0:T(128)} %dynamic_slice.7.refs_0_.length_ref, bf16[256,1024]{1,0:T(8,128)(2,1)S(1)} %multiply_convert_fusion.9.glu_ref, f32[5,1024]{1,0:T(8,128)S(1)} %convert_element_type.172.kernel_ref), custom_call_target="tpu_custom_call" | custom-call | tf_op jit(solution)/shard_map/pallas_call | solution.py:238
  91.3 2.2 fusion.36
  94.1 8.1 %multiply_convert_fusion = (bf16[256,4096]{1,0:T(8,128)(2,1)S(1)}, f32[256,4096]{1,0:T(8,128)}) fusion(bf16[256,1024]{1,0:T(8,128)(2,1)S(1)} %multiply_convert_fusion.7.refs_5_.refs_0_, bf16[1024,4096]{1,0:T(8,128)(2,1)} %param.36), kind=kOutput, calls=%fused_computation.6 | convolution fusion | flops 2152726528 | bytes 15204352 | tf_op jit(solution)/shard_map/dot_general | solution.py:52
  102.2 2.5 fusion.37
  105.5 1.2 fusion.32
  106.9 5.5 %fusion.3.refs_6_.refs_1_ = bf16[256,4096]{1,0:T(8,128)(2,1)S(1)} fusion(bf16[256,1024]{1,0:T(8,128)(2,1)S(1)} %multiply_convert_fusion.5.refs_4_, bf16[4096,1024]{1,0:T(8,128)(2,1)S(1)} %bitcast.141, f32[256,4096]{1,0:T(8,128)} %get-tuple-element.148), kind=kOutput, calls=%fused_computation.5 | convolution fusion | flops 2156920832 | bytes 15204352 | tf_op jit(solution)/shard_map/dot_general | solution.py:44
  112.3 15.5 %multiply_reduce_fusion.1 = (f32[1024]{0:T(1024)S(1)}, f32[256]{0:T(256)S(1)}, f32[256,1024]{1,0:T(8,128)S(1)}) fusion(f32[256,1024]{1,0:T(8,128)S(1)} %get-tuple-element.146, f32[256]{0:T(256)S(1)} %fusion.24, f32[256]{0:T(256)S(1)} %broadcast_multiply_fusion.5, f32[1024]{0:T(1024)S(1)} %bitcast.123, bf16[256,4096]{1,0:T(8,128)(2,1)S(1)} %fusion.3.refs_6_.refs_1_, ...), kind=kOutput, calls=%fused_computation.38 | convolution fusion | flops 2149317376 | bytes 12594176 | tf_op jit(solution)/shard_map/dot_general | solution.py:44
  130.0 14.8 %shard_map.325 = (f32[256,1024]{1,0:T(8,128)S(1)}, f32[8,1024]{1,0:T(8,128)S(1)}, f32[2,1024]{1,0:T(2,128)S(1)}) custom-call(s32[1]{0:T(128)} %dynamic_slice.7.refs_0_.length_ref, f32[1]{0:T(128)} %bitcast.22.count_ref, f32[256,1024]{1,0:T(8,128)S(1)} %fusion.4.grad_ref, f32[256,1024]{1,0:T(8,128)S(1)} %get-tuple-element.51.conv_ref, ...), custom_call_target="tpu_custom_call" | custom-call | tf_op jit(solution)/shard_map/pallas_call | solution.py:349
  145.4 1.5 multiply_reduce_fusion.2
  149.3 1.9 multiply_sine_fusion
  152.2 47.4 %shard_map.326 = (bf16[256,3072]{1,0:T(8,128)(2,1)S(1)}, bf16[256,1024]{1,0:T(8,128)(2,1)S(1)}, bf16[3,256,1024]{2,1,0:T(8,128)(2,1)S(1)}) custom-call(s32[1]{0:T(128)} %dynamic_slice.7.refs_0_.length_ref, bf16[1024,768]{1,0:T(8,128)(2,1)S(1)} %copy-done.12, bf16[256,1024]{1,0:T(8,128)(2,1)S(1)} %convolution_convert_fusion.refs_2_, ...), custom_call_target="tpu_custom_call" | custom-call | flops 2684354560 | bytes 4194304 | tf_op jit(solution)/shard_map/pallas_call | solution.py:795
  199.7 2.3 multiply_reduce_fusion.3
  203.2 1.4 slice-done.5
  204.6 1.4 copy-done.45
  206.1 3.0 fusion.2.refs_18_
  209.1 6.8 %multiply_reduce_fusion.4 = (f32[1024]{0:T(1024)S(1)}, f32[256]{0:T(256)S(1)}, f32[256,1024]{1,0:T(8,128)S(1)}) fusion(bf16[1,256,1024]{2,1,0:T(8,128)(2,1)S(1)} %copy-done.22, f32[256]{0:T(256)S(1)} %fusion.21, f32[256]{0:T(256)S(1)} %broadcast_multiply_fusion.8, f32[1024]{0:T(1024)S(1)} %bitcast.102, f32[256]{0:T(256)S(1)} %bitcast.110, ...), kind=kOutput, calls=%fused_computation.41 | convolution fusion | flops 2150365952 | bytes 12079104 | tf_op jit(solution)/shard_map/dot_general | solution.py:44
  216.6 1.1 multiply_reduce_fusion
  217.6 1.1 pad_maximum_fusion.refs_7_
  219.6 154.4 %shard_map.327 = (f32[256,512]{1,0:T(8,128)}, f32[128,1024]{1,0:T(8,128)}, f32[256,256]{1,0:T(8,128)}, f32[256,128]{1,0:T(8,128)}, f32[256,128]{1,0:T(8,128)}, /...) custom-call(bf16[256,1024]{1,0:T(8,128)(2,1)} %copy-done.7, ...), custom_call_target="tpu_custom_call" | custom-call | flops 12348030976 | bytes 419430400 | tf_op jit(solution)/shard_map/pallas_call | solution.py:1215
  374.0 3.5 shard_map.328
  (184 shorter events, 21.0 us)
Async XLA Ops:
  0.7 90.7 %copy-start = (bf16[1024,1024]{1,0:T(8,128)(2,1)S(1)}, bf16[1024,1024]{1,0:T(8,128)(2,1)}, u32[]{:S(2)}) copy-start(bf16[1024,1024]{1,0:T(8,128)(2,1)} %param.35) | copy-start | bytes 6291460
  6.5 9.6 %slice-start.2 = ((s8[8388608]{0:T(1024)(128)(4,1)}), s8[4194304]{0:T(1024)(128)(4,1)S(1)}, s32[]{:S(2)}) async-start(s8[8388608]{0:T(1024)(128)(4,1)} %bitcast.142), calls=%async_computation.2 | async-start | bytes 8388608
  8.1 22.6 %copy-start.5 = (bf16[256,1024]{1,0:T(8,128)(2,1)}, bf16[256,1024]{1,0:T(8,128)(2,1)S(1)}, u32[]{:S(2)}) copy-start(bf16[256,1024]{1,0:T(8,128)(2,1)S(1)} %multiply_convert_fusion.12.refs_4_.refs_17_) | copy-start | bytes 1572868
  8.1 8.0 %copy-start.21 = (bf16[1,256,1024]{2,1,0:T(8,128)(2,1)S(1)}, bf16[1,256,1024]{2,1,0:T(8,128)(2,1)}, u32[]{:S(2)}) copy-start(bf16[1,256,1024]{2,1,0:T(8,128)(2,1)} %param.20) | copy-start | bytes 1572868
  8.1 8.0 %slice-start.3 = ((s8[8388608]{0:T(1024)(128)(4,1)}), s8[4194304]{0:T(1024)(128)(4,1)S(1)}, s32[]{:S(2)}) async-start(s8[8388608]{0:T(1024)(128)(4,1)} %bitcast.142), calls=%async_computation.3 | async-start | bytes 8388608
  23.0 7.7 %copy-start.6 = (bf16[256,1024]{1,0:T(8,128)(2,1)}, bf16[256,1024]{1,0:T(8,128)(2,1)S(1)}, u32[]{:S(2)}) copy-start(bf16[256,1024]{1,0:T(8,128)(2,1)S(1)} %multiply_convert_fusion.11.refs_5_.refs_12_) | copy-start | bytes 1572868
  32.6 32.7 %copy-start.19 = (f32[256,1024]{1,0:T(8,128)S(1)}, f32[256,1024]{1,0:T(8,128)}, u32[]{:S(2)}) copy-start(f32[256,1024]{1,0:T(8,128)} %get-tuple-element.142) | copy-start | bytes 3145732
  32.6 32.7 %copy-start.26 = (bf16[1024,1024]{1,0:T(8,128)(2,1)S(1)}, bf16[1024,1024]{1,0:T(8,128)(2,1)}, u32[]{:S(2)}) copy-start(bf16[1024,1024]{1,0:T(8,128)(2,1)} %param.30) | copy-start | bytes 6291460
  65.2 5.0 %copy-start.4 = (bf16[256,1024]{1,0:T(8,128)(2,1)}, bf16[256,1024]{1,0:T(8,128)(2,1)S(1)}, u32[]{:S(2)}) copy-start(bf16[256,1024]{1,0:T(8,128)(2,1)S(1)} %get-tuple-element.50.refs_8_) | copy-start | bytes 1572868
  65.2 5.0 %copy-start.11 = (bf16[1024,768]{1,0:T(8,128)(2,1)}, bf16[1024,768]{1,0:T(8,128)(2,1)S(1)}, u32[]{:S(2)}) copy-start(bf16[1024,768]{1,0:T(8,128)(2,1)S(1)} %get-tuple-element.55.refs_1_) | copy-start | bytes 4718596
  65.2 5.0 %copy-start.14 = (bf16[256,1024]{1,0:T(8,128)(2,1)}, bf16[256,1024]{1,0:T(8,128)(2,1)S(1)}, u32[]{:S(2)}) copy-start(bf16[256,1024]{1,0:T(8,128)(2,1)S(1)} %get-tuple-element.60.refs_19_) | copy-start | bytes 1572868
  65.2 5.0 %copy-start.15 = (bf16[256,1024]{1,0:T(8,128)(2,1)}, bf16[256,1024]{1,0:T(8,128)(2,1)S(1)}, u32[]{:S(2)}) copy-start(bf16[256,1024]{1,0:T(8,128)(2,1)S(1)} %get-tuple-element.59.refs_14_) | copy-start | bytes 1572868
  68.9 20.7 %copy-start.37 = (bf16[1024]{0:T(1024)(128)(2,1)S(1)}, bf16[1024]{0:T(1024)(128)(2,1)}, u32[]{:S(2)}) copy-start(bf16[1024]{0:T(1024)(128)(2,1)} %param.34) | copy-start | bytes 6148
  68.9 20.7 %copy-start.38 = (bf16[1024]{0:T(1024)(128)(2,1)S(1)}, bf16[1024]{0:T(1024)(128)(2,1)}, u32[]{:S(2)}) copy-start(bf16[1024]{0:T(1024)(128)(2,1)} %param.33) | copy-start | bytes 6148
  70.2 18.4 %copy-start.23 = (f32[256,2048]{1,0:T(8,128)}, f32[256,2048]{1,0:T(8,128)S(1)}, u32[]{:S(2)}) copy-start(f32[256,2048]{1,0:T(8,128)S(1)} %fusion.39) | copy-start | bytes 6291460
  91.3 10.9 %copy-start.25 = (bf16[256,1024]{1,0:T(8,128)(2,1)}, bf16[256,1024]{1,0:T(8,128)(2,1)S(1)}, u32[]{:S(2)}) copy-start(bf16[256,1024]{1,0:T(8,128)(2,1)S(1)} %multiply_convert_fusion.8.refs_10_) | copy-start | bytes 1572868
  93.8 8.4 %slice-start = ((s8[8388608]{0:T(1024)(128)(4,1)}), s8[4194304]{0:T(1024)(128)(4,1)S(1)}, s32[]{:S(2)}) async-start(s8[8388608]{0:T(1024)(128)(4,1)} %bitcast.140), calls=%async_computation | async-start | bytes 8388608
  94.1 58.1 %copy-start.7 = (bf16[256,1024]{1,0:T(8,128)(2,1)}, bf16[256,1024]{1,0:T(8,128)(2,1)S(1)}, u32[]{:S(2)}) copy-start(bf16[256,1024]{1,0:T(8,128)(2,1)S(1)} %multiply_convert_fusion.7.refs_5_.refs_0_) | copy-start | bytes 1572868
  94.1 8.1 %slice-start.1 = ((s8[8388608]{0:T(1024)(128)(4,1)}), s8[4194304]{0:T(1024)(128)(4,1)S(1)}, s32[]{:S(2)}) async-start(s8[8388608]{0:T(1024)(128)(4,1)} %bitcast.140), calls=%async_computation.1 | async-start | bytes 8388608
  106.8 5.5 %copy-start.33 = (bf16[256,1024]{1,0:T(8,128)(2,1)}, bf16[256,1024]{1,0:T(8,128)(2,1)S(1)}, u32[]{:S(2)}) copy-start(bf16[256,1024]{1,0:T(8,128)(2,1)S(1)} %multiply_convert_fusion.5.refs_4_) | copy-start | bytes 1572868
  112.3 39.8 %copy-start.10 = (bf16[256,4096]{1,0:T(8,128)(2,1)}, bf16[256,4096]{1,0:T(8,128)(2,1)S(1)}, u32[]{:S(2)}) copy-start(bf16[256,4096]{1,0:T(8,128)(2,1)S(1)} %fusion.3.refs_6_.refs_1_) | copy-start | bytes 6291460
  128.5 16.3 %copy-start.24 = (f32[256,2048]{1,0:T(8,128)S(1)}, f32[256,2048]{1,0:T(8,128)}, u32[]{:S(2)}) copy-start(f32[256,2048]{1,0:T(8,128)} %copy-done.23) | copy-start | bytes 6291460
  129.6 15.8 %copy-start.18 = (f32[256,1024]{1,0:T(8,128)S(1)}, f32[256,1024]{1,0:T(8,128)}, u32[]{:S(2)}) copy-start(f32[256,1024]{1,0:T(8,128)} %copy-done.17) | copy-start | bytes 3145732
  129.6 15.8 %copy-start.40 = (bf16[1024,2048]{1,0:T(8,128)(2,1)S(1)}, bf16[1024,2048]{1,0:T(8,128)(2,1)}, u32[]{:S(2)}) copy-start(bf16[1024,2048]{1,0:T(8,128)(2,1)} %param.31) | copy-start | bytes 12582916
  151.6 48.1 %slice-start.6 = ((s8[6291456]{0:T(1024)(128)(4,1)}), s8[4194304]{0:T(1024)(128)(4,1)S(1)}, s32[]{:S(2)}) async-start(s8[6291456]{0:T(1024)(128)(4,1)} %bitcast.146), calls=%async_computation.6 | async-start | bytes 8388608
  152.2 47.5 %copy-start.20 = (f32[256,1024]{1,0:T(8,128)S(1)}, f32[256,1024]{1,0:T(8,128)}, u32[]{:S(2)}) copy-start(f32[256,1024]{1,0:T(8,128)} %get-tuple-element.142) | copy-start | bytes 3145732
  152.2 47.5 %slice-start.7 = ((s8[6291456]{0:T(1024)(128)(4,1)}), s8[2097152]{0:T(1024)(128)(4,1)S(1)}, s32[]{:S(2)}) async-start(s8[6291456]{0:T(1024)(128)(4,1)} %bitcast.146), calls=%async_computation.7 | async-start | bytes 4194304
  202.8 6.3 %copy-start.31 = (bf16[256,1024]{1,0:T(8,128)(2,1)}, bf16[256,1024]{1,0:T(8,128)(2,1)S(1)}, u32[]{:S(2)}) copy-start(bf16[256,1024]{1,0:T(8,128)(2,1)S(1)} %get-tuple-element.101.refs_15_) | copy-start | bytes 1572868
  209.1 6.8 %copy-start.42 = (bf16[256,4096]{1,0:T(8,128)(2,1)}, bf16[256,4096]{1,0:T(8,128)(2,1)S(1)}, u32[]{:S(2)}) copy-start(bf16[256,4096]{1,0:T(8,128)(2,1)S(1)} %fusion.2.refs_18_) | copy-start | bytes 6291460
  219.6 158.5 %copy-start.35 = (f32[1024]{0:T(1024)S(1)}, f32[1024]{0:T(1024)}, u32[]{:S(2)}) copy-start(f32[1024]{0:T(1024)} %param.38) | copy-start | bytes 12292
  219.6 159.1 %copy-start.36 = (f32[1024]{0:T(1024)S(1)}, f32[1024]{0:T(1024)}, u32[]{:S(2)}) copy-start(f32[1024]{0:T(1024)} %param.39) | copy-start | bytes 12292
  219.6 159.7 %copy-start.1 = (bf16[1024,1024]{1,0:T(8,128)(2,1)S(1)}, bf16[1024,1024]{1,0:T(8,128)(2,1)}, u32[]{:S(2)}) copy-start(bf16[1024,1024]{1,0:T(8,128)(2,1)} %param.35) | copy-start | bytes 6291460
  (22 other events, 57.2 us)
